TPU v7x, 256 devices: a whole 4x4x8 slice. The times are simulated.
256 devices in a mesh: dp: 64 (over z, x_hi, y), mp: 4 (over x_lo, core).
Axes of the slice: x: 4 (x_hi: 2, x_lo: 2; x = x_hi * 2 + x_lo), y: 4, z: 8, core: 2. Of those that a mesh axis runs over, the one named last changes fastest.
Arguments:
- teacher_in: bfloat16 [16384, 1024], P('dp'), may hold values from -6 to 6
- teacher_fc1: bfloat16 [1024, 4096], P(None, 'mp'), may hold values from -0.1875 to 0.1875
- teacher_fc2: bfloat16 [4096, 1024], P('mp'), may hold values from -0.09375 to 0.09375
- tok_in: bfloat16 [16384, 768], P('dp', 'mp'), may hold values from -6 to 6
- enc_proj: bfloat16 [768, 32], P('mp'), may hold values from -0.21875 to 0.21875
- codes: int32 [16384], P('dp'), may hold values from 0 to 8191
- ema_count: float32 [8192], replicated, may hold values from 0.5 to 8
- ema_sum: float32 [32, 8192], replicated, may hold values from -6 to 6
- dec_in: bfloat16 [32, 768], replicated, may hold values from -1 to 1
- head: bfloat16 [768, 1024], P(None, 'mp'), may hold values from -0.21875 to 0.21875
Outputs:
- new_count: float32 [8192], replicated
- new_sum: float32 [32, 8192], replicated
- grad_head: float32 [768, 1024], P(None, 'mp')
- grad_dec: float32 [32, 768], replicated
- grad_enc: float32 [768, 32], P('mp')
All inputs are finite; a program needn't handle non-finite values.
Results may differ from a plain program's by a relative error of at most 0.015.
Values may be sent and summed in bfloat16 or wider, within the bound.
A program may use at most 64 MiB of HBM per device.

v0:
```python
import jax
import jax.numpy as jnp
from jax import lax
from jax.sharding import PartitionSpec as P

DECAY = 0.5
BETA = 0.25
EPS = 1e-06


def split_three(values):
    upper = values.astype(jnp.bfloat16)
    rest = values - upper.astype(jnp.float32)
    middle = rest.astype(jnp.bfloat16)
    lower = (rest - middle.astype(jnp.float32)).astype(jnp.bfloat16)
    return (upper, middle, lower)


def code_blocks(codes, z, codebook):
    total = codebook.shape[1]
    width = min(1024, total)
    blocks = total // width
    books = codebook.reshape(codebook.shape[0], blocks, width).transpose(1, 0, 2)
    z_parts = split_three(z)

    def step(carry, inputs):
        block, book = inputs
        ids = block * width + jnp.arange(width, dtype=jnp.int32)
        onehot = (codes[:, None] == ids[None, :]).astype(jnp.bfloat16)
        looked = jnp.zeros_like(carry)
        for part in split_three(book):
            looked = looked + lax.dot_general(
                onehot, part, (((1,), (1,)), ((), ())), preferred_element_type=jnp.float32
            )
        sums = jnp.zeros((z.shape[1], width), jnp.float32)
        for part in z_parts:
            sums = sums + lax.dot_general(
                part, onehot, (((0,), (0,)), ((), ())), preferred_element_type=jnp.float32
            )
        counts = jnp.sum(onehot.astype(jnp.float32), axis=0)
        return (carry + looked, (counts, sums))

    start = jnp.zeros((z.shape[0], codebook.shape[0]), jnp.float32)
    quant, (counts, sums) = lax.scan(step, start, (jnp.arange(blocks, dtype=jnp.int32), books))
    return (quant, counts.reshape(total), sums.transpose(1, 0, 2).reshape(codebook.shape[0], total))


def on_device(
    teacher_in, teacher_fc1, teacher_fc2, tok_in, enc_proj, codes, ema_count, ema_sum, dec_in, head
):
    teacher_hidden = jax.nn.gelu(
        jnp.dot(teacher_in, teacher_fc1, preferred_element_type=jnp.float32)
    ).astype(jnp.bfloat16)
    partial_value = jnp.dot(teacher_hidden, teacher_fc2, preferred_element_type=jnp.float32)
    teacher_share = lax.psum_scatter(
        partial_value.astype(jnp.bfloat16), "mp", scatter_dimension=1, tiled=True
    ).astype(jnp.float32)
    columns = head.shape[1]
    own_cols = lax.dynamic_slice_in_dim(teacher_in, lax.axis_index("mp") * columns, columns, 1)
    target = teacher_share + own_cols.astype(jnp.float32)
    z = lax.psum(
        jnp.dot(tok_in, enc_proj, preferred_element_type=jnp.float32).astype(jnp.bfloat16), "mp"
    ).astype(jnp.float32)
    codebook = ema_sum / ema_count[None, :]
    own_rows = z.shape[0] // lax.axis_size("mp")
    row_start = lax.axis_index("mp") * own_rows
    my_codes = lax.dynamic_slice_in_dim(codes, row_start, own_rows, 0)
    my_z = lax.dynamic_slice_in_dim(z, row_start, own_rows, 0)
    quant_part, batch_count, batch_sum = code_blocks(my_codes, my_z, codebook)
    quant = lax.all_gather(quant_part, "mp", axis=0, tiled=True)
    total_count, total_sum = lax.psum((batch_count, batch_sum), ("dp", "mp"))
    new_count = DECAY * ema_count + (1.0 - DECAY) * total_count
    new_sum = DECAY * ema_sum + (1.0 - DECAY) * total_sum
    q_round = quant.astype(jnp.bfloat16)
    pre = jnp.dot(q_round, dec_in, preferred_element_type=jnp.float32)
    hidden = jax.nn.gelu(pre).astype(jnp.bfloat16)
    pred = jnp.dot(hidden, head, preferred_element_type=jnp.float32)
    pp, pt, tt = lax.psum(
        (
            jnp.sum(pred * pred, axis=1),
            jnp.sum(pred * target, axis=1),
            jnp.sum(target * target, axis=1),
        ),
        "mp",
    )
    norm_p = jnp.sqrt(pp + EPS)
    norm_t = jnp.sqrt(tt + EPS)
    dpred = (
        -target / (norm_p * norm_t)[:, None] + (pt / (norm_p**3 * norm_t))[:, None] * pred
    ).astype(jnp.bfloat16)
    local_head = lax.dot_general(
        hidden, dpred, (((0,), (0,)), ((), ())), preferred_element_type=jnp.float32
    )
    dh_part = lax.dot_general(
        dpred, head, (((1,), (1,)), ((), ())), preferred_element_type=jnp.float32
    )
    dh = lax.psum(dh_part.astype(jnp.bfloat16), "mp").astype(jnp.float32)
    dpre = jax.vjp(jax.nn.gelu, pre)[1](dh)[0].astype(jnp.bfloat16)
    local_dec = lax.dot_general(
        q_round, dpre, (((0,), (0,)), ((), ())), preferred_element_type=jnp.float32
    )
    dq = lax.dot_general(dpre, dec_in, (((1,), (1,)), ((), ())), preferred_element_type=jnp.float32)
    dz = (dq + 2.0 * BETA * (z - quant)).astype(jnp.bfloat16)
    local_enc = lax.dot_general(
        tok_in, dz, (((0,), (0,)), ((), ())), preferred_element_type=jnp.float32
    )
    grad_head, grad_dec, grad_enc = lax.psum((local_head, local_dec, local_enc), "dp")
    return (new_count, new_sum, grad_head, grad_dec, grad_enc)


def solution(mesh):
    placed = (
        P("dp", None),
        P(None, "mp"),
        P("mp", None),
        P("dp", "mp"),
        P("mp", None),
        P("dp"),
        P(),
        P(),
        P(),
        P(None, "mp"),
    )
    return jax.shard_map(
        on_device,
        mesh=mesh,
        in_specs=placed,
        out_specs=(P(), P(), P(None, "mp"), P(), P("mp", None)),
        check_vma=False,
    )
```

profile of v0, /device:TPU:2, one launch (start us, length us, event | category | flops | bytes accessed | tf_op | source)
XLA Modules:
  0.0 1096.6 jit_solution(11893163592988038881)
XLA Ops:
  7.3 1.5 copy-done
  8.8 4.1 convolution_convert_fusion
  13.1 10.2 psum.70
  23.8 1.6 copy.48
  25.4 49.6 %while.15 = (s32[]{:T(128)}, f32[64,32]{0,1:T(8,128)S(1)}, f32[8,1024]{1,0:T(8,128)}, f32[8,32,1024]{2,1,0:T(8,128)}, s32[64]{0:T(128)S(1)}, /*index=5*/s32[8]{0...) while((s32[]{:T(128)}, f32[64,32]{0,1:T(8,128)S(1)}, ...), condition=%wide.region_3.4_spmd.clone, body=%wide.region_1.3_spmd.clone.sunk | while | flops 26255364 | bytes 1419691 | solution.py:44
  27.2 0.9 fusion.119
  28.1 1.3 constant_dynamic-slice_fusion.2
  30.2 1.4 dynamic_update_slice.14
  33.4 0.9 fusion.119
  34.3 1.3 constant_dynamic-slice_fusion.2
  36.4 1.4 dynamic_update_slice.14
  39.6 0.9 fusion.119
  40.5 1.3 constant_dynamic-slice_fusion.2
  42.7 1.4 dynamic_update_slice.14
  45.8 0.9 fusion.119
  46.7 1.3 constant_dynamic-slice_fusion.2
  48.9 1.4 dynamic_update_slice.14
  52.0 0.9 fusion.119
  52.9 1.3 constant_dynamic-slice_fusion.2
  55.1 1.4 dynamic_update_slice.14
  58.2 0.9 fusion.119
  59.1 1.3 constant_dynamic-slice_fusion.2
  61.3 1.4 dynamic_update_slice.14
  64.4 0.9 fusion.119
  65.3 1.3 constant_dynamic-slice_fusion.2
  67.5 1.4 dynamic_update_slice.14
  70.6 0.9 fusion.119
  71.5 1.3 constant_dynamic-slice_fusion.2
  73.7 1.4 dynamic_update_slice.14
  75.1 5.4 all-gather
  81.8 2.2 multiply_reduce_fusion.2
  84.0 1.1 copy.44
  85.1 1.1 multiply_reduce_fusion.1
  86.2 7.6 all-reduce.1
  93.9 1.1 add_convert_fusion
  95.0 2.1 convolution_convert_fusion.1
  97.2 2.4 copy.47
  99.6 78.4 %psum.71 = f32[8192]{0:T(1024)S(1)} all-reduce(f32[8192]{0:T(1024)S(1)} %bitcast.81), channel_id=1, replica_groups=mesh['dp'=64,'mp'=4] {'dp','mp'}, use_global_device_ids=true, to_apply=%region_4.5 | all-reduce | flops 8192 | bytes 65536 | tf_op jit(solution)/shard_map/psum | solution.py:71
  178.6 2.5 fusion.68
  181.1 1.8 fusion.38
  183.0 1.6 fusion.55
  184.6 220.3 %all-reduce.6.cloned.1.call-done = f32[32,8192]{1,0:T(8,128)} async-done(((f32[32,8192]{1,0:T(8,128)}), f32[32,8192]{1,0:T(8,128)}) %all-reduce.6.cloned.1.call-update) | async-done | bytes 1048592 | tf_op jit(solution)/shard_map/psum | solution.py:71
  404.9 2.3 add_multiply_fusion
  407.2 1.3 convolution_bitcast_fusion
  408.5 353.7 %psum.79 = f32[192,32]{0,1:T(8,128)} all-reduce(f32[192,32]{0,1:T(8,128)S(1)} %convolution_bitcast_fusion), channel_id=1, replica_groups=mesh['dp'=64,'mp'=4] {'dp'}, use_global_device_ids=true, to_apply=%region_16.17 | all-reduce | flops 6144 | bytes 49152 | tf_op jit(solution)/shard_map/psum | solution.py:107
  762.2 324.3 %all-reduce.10.cloned.1.call-done = (f32[768,256]{1,0:T(8,128)}, f32[32,768]{1,0:T(8,128)}) async-done(((f32[768,256]{1,0:T(8,128)}, f32[32,768]{1,0:T(8,128)}), (f32[768,256]{1,0:T(8,128)}, f32[32,768]{1,0:T(8,128)})) %all-reduce.10.cloned.1.call-update) | async-done | bytes 884752 | tf_op jit(solution)/shard_map/psum | solution.py:107
  1086.5 2.1 copy.92
  1088.5 1.5 copy.93
  (113 shorter events, 18.1 us)
Async XLA Ops:
  7.2 1.6 copy-start
  7.2 5.7 copy-start.4
  7.2 5.7 copy-start.9
  7.2 16.4 %copy-start.10 = (s32[256]{0:T(256)S(1)}, s32[256]{0:T(256)}, u32[]{:S(2)}) copy-start(s32[256]{0:T(256)} %param.17) | copy-start | bytes 3076
  7.2 16.5 %copy-start.6 = (f32[8192]{0:T(1024)S(1)}, f32[8192]{0:T(1024)}, u32[]{:S(2)}) copy-start(f32[8192]{0:T(1024)} %param.18) | copy-start | bytes 98308
  7.2 16.5 %copy-start.1 = (f32[32,8192]{1,0:T(8,128)S(1)}, f32[32,8192]{1,0:T(8,128)}, u32[]{:S(2)}) copy-start(f32[32,8192]{1,0:T(8,128)} %param.19) | copy-start | bytes 3145732
  7.2 77.9 %reduce-scatter.2.cloned.1.call-start = ((), (), s32[]{:S(2)}) async-start(), calls=%async_computation.2 | async-start | bytes 655360 | tf_op jit(solution)/shard_map/reduce_scatter | solution.py:55
  12.8 168.3 %all-reduce.8.cloned.1.call-start = ((), (), s32[]{:S(2)}) async-start(), calls=%async_computation.3 | async-start | bytes 786432 | tf_op jit(solution)/shard_map/psum | solution.py:97
  25.4 55.2 %copy-start.5 = (bf16[32,768]{1,0:T(8,128)(2,1)S(1)}, bf16[32,768]{1,0:T(8,128)(2,1)}, u32[]{:S(2)}) copy-start(bf16[32,768]{1,0:T(8,128)(2,1)} %param.20) | copy-start | bytes 147460
  80.7 3.3 copy-start.3
  80.9 0.9 copy-start.2
  95.0 4.6 copy-start.8
  95.0 83.0 %copy-start.7 = (f32[8192]{0:T(1024)S(1)}, f32[8192]{0:T(1024)}, u32[]{:S(2)}) copy-start(f32[8192]{0:T(1024)} %param.18) | copy-start | bytes 98308
  97.1 307.8 %all-reduce.6.cloned.1.call-start = ((), (), s32[]{:S(2)}) async-start(), calls=%async_computation.1 | async-start | bytes 2097152 | tf_op jit(solution)/shard_map/psum | solution.py:71
  99.6 986.9 %all-reduce.10.cloned.1.call-start = ((), (), s32[]{:S(2)}) async-start(), calls=%async_computation.4 | async-start | bytes 1769472 | tf_op jit(solution)/shard_map/psum | solution.py:107
Sparse Core Ops, SparseCore 0:
  13.0 22.3 reduce-scatter.1
  97.2 43.4 all-reduce.7
  147.1 257.7 all-reduce.5
  408.0 678.4 all-reduce.9
where the time goes:
time: 1100 us
  waiting for transfers between devices  545 us (50%)
  blocking collectives  455 us (41%)
  local copies, waits for them, and re-layouts  38 us (3%)
  matrix products  31 us (3%)
  between operations  14 us (1%)
    psum x1, blocking collectives, on_device(): lax.psum((local_head, local_dec, local_enc), 'dp')  354 us
    psum x1, waiting for transfers between devices, on_device(): lax.psum((local_head, local_dec, local_enc), 'dp')  324 us
    psum x1, waiting for transfers between devices, on_device(): total_count, total_sum = lax.psum((batch_count, batch_sum), ('dp', 'mp'))  220 us
    psum x1, blocking collectives, on_device(): total_count, total_sum = lax.psum((batch_count, batch_sum), ('dp', 'mp'))  78.4 us
  transfers between devices with their start and end apart: 4, of which 2 were waited for; matrix products, arithmetic and copies ran while one was open for 6% of the time, Pallas kernels for 0%

commit v1 on v0

v1 whole, which is shorter than its diff:
```python
import functools
import math

import jax
import jax.numpy as jnp
from jax import lax
from jax.experimental import pallas as pl
from jax.experimental.pallas import tpu as pltpu
from jax.sharding import PartitionSpec as P

DECAY = 0.5
BETA = 0.25
EPS = 1e-06
MESH = pl.DeviceIdType.MESH
F32 = jnp.float32
BF16 = jnp.bfloat16
GELU_A = math.sqrt(2.0 / math.pi)
GELU_B = 0.044715

NMP = 4
GRP = 8
ZED = 8
ROWS = 256
OWN = 64
HI = 64
QHI = 16
SROW = 64
CROW = 16
GH = 96
GX = 16


def gelu(x):
    return 0.5 * x * (1.0 + jnp.tanh(GELU_A * (x + GELU_B * (x * x * x))))


def gelu_and_slope(x):
    square = x * x
    t = jnp.tanh(GELU_A * (x + GELU_B * (square * x)))
    value = 0.5 * x * (1.0 + t)
    slope = 0.5 * (1.0 + t) + (0.5 * GELU_A) * x * (1.0 - t * t) * (
        1.0 + (3.0 * GELU_B) * square
    )
    return value, slope


def dot(a, b, ca=1, cb=0):
    return lax.dot_general(a, b, (((ca,), (cb,)), ((), ())), preferred_element_type=F32)


def kernel(
    tin_h, fc1_h, fc2_h, tok_h, enc_h, codes_h, cnt_h, sum_h, dec_h, head_h,
    ncount_h, nsum_h, ghead_h, gdec_h, genc_h,
    tin, fc1, fc2, tok, enc, codes, cnt, inv, esum, dec,
    th, tp, hid_t, q_rows, book, pred,
    hd, tp_r, z_s, z_r, s_s, s_r, s_z, s_all, dp_s, dp_r, dpre, g_s, g_r, g_z, g_all,
    o_count, o_sum, o_head, o_dec, o_enc,
    load_sem, out_sem,
    hd_ss, hd_rs, tp_ss, tp_rs, z_ss, z_rs, s1_ss, s1_rs, s2_ss, s2_rs, s3_ss, s3_rs,
    s4_ss, s4_rs, dp_ss, dp_rs, dr_ss, dr_rs, g1_ss, g1_rs, x1_ss, x1_rs, g2_ss, g2_rs,
    g3_ss, g3_rs,
):
    dp = lax.axis_index("dp")
    mp = lax.axis_index("mp")
    zed = lax.div(dp, GRP)
    grp = lax.rem(dp, GRP)
    sib = mp + 1 - 2 * lax.rem(mp, 2)
    over = lax.rem(mp + 2, NMP)
    sib_over = lax.rem(sib + 2, NMP)

    def mp_peer(r):
        return (dp, lax.rem(mp + r, NMP))

    def grp_index(k):
        return lax.rem(grp + k, GRP)

    def grp_peer(k):
        return (zed * GRP + grp_index(k), mp)

    def zed_peer(k):
        return (lax.rem(zed + k, ZED) * GRP + grp, mp)

    wrap = (zed * GRP + grp_index(4), over)

    def remote(src, dst, ss, rs, dev):
        return pltpu.make_async_remote_copy(
            src_ref=src, dst_ref=dst, send_sem=ss, recv_sem=rs,
            device_id=dev, device_id_type=MESH,
        )

    barrier = pltpu.get_barrier_semaphore()
    peers = [mp_peer(r) for r in (1, 2, 3)] + [wrap]
    peers += [grp_peer(k) for k in range(1, GRP)] + [zed_peer(k) for k in range(1, ZED)]
    for dev in peers:
        pl.semaphore_signal(barrier, inc=1, device_id=dev, device_id_type=MESH)

    loads = []

    def load(src, dst):
        c = pltpu.make_async_copy(src, dst, load_sem.at[len(loads)])
        c.start()
        loads.append(c)
        return c

    l_tok = load(tok_h, tok)
    l_enc = load(enc_h, enc)
    l_tin = load(tin_h, tin)
    l_fc1 = [load(fc1_h.at[:, pl.ds(n * 256, 256)], fc1.at[n]) for n in range(4)]
    l_head = load(head_h, hd.at[mp])
    l_fc2 = [load(fc2_h.at[:, pl.ds(n * 256, 256)], fc2.at[n]) for n in range(4)]
    l_codes = load(codes_h, codes)
    l_cnt = load(cnt_h, cnt)
    l_sum = load(sum_h, esum)
    l_dec = load(dec_h, dec)

    l_tok.wait()
    l_enc.wait()
    z_part = dot(tok[...], enc[...])
    z_s[...] = z_part.T.astype(BF16)

    l_tin.wait()
    for n in range(4):
        l_fc1[n].wait()
        th[:, n * 256:(n + 1) * 256] = gelu(dot(tin[...], fc1[n])).astype(BF16)

    l_head.wait()
    pl.semaphore_wait(barrier, len(peers))

    c_z = [
        remote(z_s, z_r.at[r - 1], z_ss.at[r - 1], z_rs.at[r - 1], mp_peer(r)) for r in (1, 2, 3)
    ]
    for c in c_z:
        c.start()
    c_wrap = remote(hd.at[mp], hd.at[mp], hd_ss.at[0], hd_rs.at[0], wrap)
    c_wrap.start()
    c_sib = remote(hd.at[mp], hd.at[mp], hd_ss.at[1], hd_rs.at[1], (dp, sib))
    c_sib.start()

    c_tp = []
    for n in range(4):
        l_fc2[n].wait()
        tp[n] = dot(th[...], fc2[n]).astype(BF16)
        for r in (2, 1, 3):
            rows = pl.ds(pl.multiple_of(lax.rem(mp + r, NMP) * OWN, OWN), OWN)
            c = remote(
                tp.at[n, rows], tp_r.at[r - 1, n], tp_ss.at[n, r - 1], tp_rs.at[n, r - 1],
                mp_peer(r),
            )
            c.start()
            c_tp.append(c)

    l_codes.wait()
    l_cnt.wait()
    l_sum.wait()
    l_dec.wait()
    code = jnp.broadcast_to(codes[...], (32, ROWS))
    code_hi = jnp.right_shift(code, 7)
    code_lo = jnp.broadcast_to(jnp.bitwise_and(codes[...], 127), (128, ROWS))
    lo_id = lax.broadcasted_iota(jnp.int32, (128, ROWS), 0)
    lo_hot = jnp.where(lo_id == code_lo, 1.0, 0.0).astype(BF16)
    inv[...] = 1.0 / cnt[...]

    def look(i, total):
        for j in range(8):
            h = i * 8 + j
            part = esum[:, pl.ds(pl.multiple_of(h * 128, 128), 128)] * inv[pl.ds(h, 1), :]
            upper = part.astype(BF16)
            book[j * 32:(j + 1) * 32, 0:128] = upper
            book[j * 32:(j + 1) * 32, 128:256] = (part - upper.astype(F32)).astype(BF16)
        found = dot(book[...], jnp.concatenate([lo_hot, lo_hot], axis=0))
        for j in range(8):
            total = total + jnp.where(code_hi == i * 8 + j, found[j * 32:(j + 1) * 32], 0.0)
        return total

    q_t = lax.fori_loop(0, HI // 8, look, jnp.zeros((32, ROWS), F32))
    q_rows[...] = q_t.T
    q_round_t = q_t.astype(BF16)

    for c in c_z:
        c.wait()
    z_t = z_s[...].astype(F32)
    for r in range(3):
        z_t = z_t + z_r[r].astype(F32)
    z_upper = z_t.astype(BF16).astype(F32)
    z_lower = z_t - z_upper
    for i in range(QHI // 2):
        halves = []
        for part in (z_upper, z_lower):
            for j in range(2):
                halves.append(jnp.where(code_hi == mp * QHI + i * 2 + j, part, 0.0))
        both = dot(jnp.concatenate(halves, axis=0).astype(BF16), lo_hot, 1, 1)
        s_s[i, 0:SROW] = both[0:SROW] + both[SROW:2 * SROW]
    hi_id = lax.broadcasted_iota(jnp.int32, (CROW, ROWS), 0) + mp * QHI
    hi_hot = jnp.where(hi_id == code_hi[0:CROW], 1.0, 0.0).astype(BF16)
    counts = dot(hi_hot, lo_hot, 1, 1)
    for i in range(GRP):
        s_s[i, SROW:SROW + CROW] = counts
    c_s1 = []
    for k in (6, 2, 5, 7, 4, 1, 3):
        c = remote(
            s_s.at[grp_index(k)], s_r.at[k - 1], s1_ss.at[k - 1], s1_rs.at[k - 1], grp_peer(k)
        )
        c.start()
        c_s1.append(c)

    dec_t = dec[...].astype(F32).T.astype(BF16)
    for n in range(3):
        hid_t[n * 256:(n + 1) * 256, :] = gelu(
            dot(dec_t[n * 256:(n + 1) * 256], q_round_t)
        ).astype(BF16)
    own_rows = pl.ds(pl.multiple_of(mp * OWN, OWN), OWN)
    hidden, slope = gelu_and_slope(dot(q_rows[own_rows, :].astype(BF16), dec[...]))
    hidden = hidden.astype(BF16)

    c_wrap.wait()
    c_fwd = remote(hd.at[over], hd.at[over], hd_ss.at[2], hd_rs.at[2], (dp, sib))
    c_fwd.start()
    c_sib.wait()
    for b in (mp, sib, over):
        pred[b] = dot(hidden, hd[b])
    c_fwd.wait()
    pred[sib_over] = dot(hidden, hd[sib_over])

    for c in c_tp:
        c.wait()
    target = []
    for n in range(4):
        t = tin[own_rows, n * 256:(n + 1) * 256].astype(F32) + tp[n, own_rows, :].astype(F32)
        for r in range(3):
            t = t + tp_r[r, n].astype(F32)
        target.append(t)
    pp = jnp.zeros((OWN, 256), F32)
    pt = jnp.zeros((OWN, 256), F32)
    tt = jnp.zeros((OWN, 256), F32)
    for n in range(4):
        pp = pp + pred[n] * pred[n]
        pt = pt + pred[n] * target[n]
        tt = tt + target[n] * target[n]
    pp = jnp.sum(pp, axis=1, keepdims=True) + EPS
    pt = jnp.sum(pt, axis=1, keepdims=True)
    tt = jnp.sum(tt, axis=1, keepdims=True) + EPS
    inverse = 1.0 / (jnp.sqrt(pp) * jnp.sqrt(tt))
    scale = pt * inverse / pp
    for n in range(4):
        dp_s[n] = (scale * pred[n] - inverse * target[n]).astype(BF16)
    c_dp = []
    for r in (2, 1, 3):
        c = remote(
            dp_s.at[lax.rem(mp + r, NMP)], dp_r.at[mp], dp_ss.at[r - 1], dp_rs.at[r - 1],
            mp_peer(r),
        )
        c.start()
        c_dp.append(c)
    dp_r[mp] = dp_s[mp]
    dh = dot(dp_s[0], hd[0], 1, 1)
    for n in range(1, 4):
        dh = dh + dot(dp_s[n], hd[n], 1, 1)
    dpre[mp] = (dh * slope).astype(BF16)
    c_dr = []
    for r in (2, 1, 3):
        c = remote(dpre.at[mp], dpre.at[mp], dr_ss.at[r - 1], dr_rs.at[r - 1], mp_peer(r))
        c.start()
        c_dr.append(c)

    for c in c_s1:
        c.wait()
    s_part = s_s[grp]
    for k in range(GRP - 1):
        s_part = s_part + s_r[k]
    s_z[zed] = s_part
    c_s2 = []
    for k in (4, 3, 5, 2, 6, 1, 7):
        c = remote(s_z.at[zed], s_z.at[zed], s2_ss.at[k - 1], s2_rs.at[k - 1], zed_peer(k))
        c.start()
        c_s2.append(c)

    for c in c_dp:
        c.wait()
    grad = dot(hid_t[...], dp_r[...].reshape(ROWS, 256)).astype(BF16)
    for i in range(GRP):
        g_s[i, 0:GH] = grad[i * GH:(i + 1) * GH]
    c_g1 = []
    for k in (6, 2, 5, 7, 4, 1, 3):
        c = remote(
            g_s.at[grp_index(k), pl.ds(0, GH)], g_r.at[k - 1, pl.ds(0, GH)],
            g1_ss.at[k - 1], g1_rs.at[k - 1], grp_peer(k),
        )
        c.start()
        c_g1.append(c)

    for c in c_dr:
        c.wait()
    dpre_all = dpre[...].reshape(ROWS, 768)
    dq_t = dot(dec[...], dpre_all, 1, 1)
    dz_t = (dq_t + 2.0 * BETA * (z_t - q_t)).astype(BF16)
    grad_dec = dot(q_round_t, dpre_all).astype(BF16)
    grad_enc = dot(dz_t, tok[...]).astype(BF16)
    for n in range(3):
        for i in range(2):
            g_s[n * 2 + i, GH:GH + GX] = grad_dec[i * 16:(i + 1) * 16, n * 256:(n + 1) * 256]
    for i in range(2):
        g_s[6 + i, GH:GH + GX, 0:192] = grad_enc[i * 16:(i + 1) * 16]
        g_s[6 + i, GH:GH + GX, 192:256] = jnp.zeros((GX, 64), BF16)
    c_x1 = []
    for k in (6, 2, 5, 7, 4, 1, 3):
        c = remote(
            g_s.at[grp_index(k), pl.ds(GH, GX)], g_r.at[k - 1, pl.ds(GH, GX)],
            x1_ss.at[k - 1], x1_rs.at[k - 1], grp_peer(k),
        )
        c.start()
        c_x1.append(c)

    for c in c_s2:
        c.wait()
    s_part = s_z[0]
    for k in range(1, ZED):
        s_part = s_part + s_z[k]
    own_part = pl.ds(pl.multiple_of(grp * SROW, SROW), SROW)
    s_all[mp, own_part] = s_part[0:SROW]
    s_all[mp, pl.ds(GRP * SROW, CROW)] = s_part[SROW:SROW + CROW]
    c_s3 = []
    for k in (6, 2, 5, 7, 4, 1, 3):
        c = remote(
            s_all.at[mp, own_part], s_all.at[mp, own_part], s3_ss.at[k - 1], s3_rs.at[k - 1],
            grp_peer(k),
        )
        c.start()
        c_s3.append(c)

    for c in c_g1 + c_x1:
        c.wait()
    g_part = g_s[grp].astype(F32)
    for k in range(GRP - 1):
        g_part = g_part + g_r[k].astype(F32)
    g_z[zed] = g_part.astype(BF16)
    c_g2 = []
    for k in (4, 3, 5, 2, 6, 1, 7):
        c = remote(g_z.at[zed], g_z.at[zed], g2_ss.at[k - 1], g2_rs.at[k - 1], zed_peer(k))
        c.start()
        c_g2.append(c)

    for c in c_s3:
        c.wait()
    c_over = remote(s_all.at[mp], s_all.at[mp], s4_ss.at[0], s4_rs.at[0], (dp, over))
    c_over.start()
    c_near = remote(s_all.at[mp], s_all.at[mp], s4_ss.at[1], s4_rs.at[1], (dp, sib))
    c_near.start()
    c_over.wait()
    c_last = remote(s_all.at[over], s_all.at[over], s4_ss.at[2], s4_rs.at[2], (dp, sib))
    c_last.start()

    for c in c_g2:
        c.wait()
    g_part = g_z[0].astype(F32)
    for k in range(1, ZED):
        g_part = g_part + g_z[k].astype(F32)
    g_all[grp] = g_part.astype(BF16)
    c_g3 = []
    for k in (6, 2, 5, 7, 4, 1, 3):
        c = remote(g_all.at[grp], g_all.at[grp], g3_ss.at[k - 1], g3_rs.at[k - 1], grp_peer(k))
        c.start()
        c_g3.append(c)

    c_near.wait()
    c_last.wait()
    for m in range(NMP):
        o_count[m * CROW:(m + 1) * CROW] = s_all[m, GRP * SROW:GRP * SROW + CROW]
        for i in range(QHI):
            columns = slice((m * QHI + i) * 128, (m * QHI + i + 1) * 128)
            o_sum[:, columns] = DECAY * esum[:, columns] + (1.0 - DECAY) * s_all[
                m, i * 32:(i + 1) * 32
            ]
    o_count[...] = DECAY * cnt[...] + (1.0 - DECAY) * o_count[...]
    outs = []

    def store(src, dst):
        c = pltpu.make_async_copy(src, dst, out_sem.at[len(outs)])
        c.start()
        outs.append(c)

    store(o_count, ncount_h)
    store(o_sum, nsum_h)

    for c in c_g3:
        c.wait()
    for i in range(GRP):
        o_head[i * GH:(i + 1) * GH] = g_all[i, 0:GH].astype(F32)
    store(o_head, ghead_h)
    for n in range(3):
        for i in range(2):
            o_dec[i * 16:(i + 1) * 16, n * 256:(n + 1) * 256] = g_all[
                n * 2 + i, GH:GH + GX
            ].astype(F32)
    store(o_dec, gdec_h)
    enc_t = jnp.concatenate(
        [g_all[6, GH:GH + GX].astype(F32), g_all[7, GH:GH + GX].astype(F32)], axis=0
    )
    o_enc[...] = enc_t[:, 0:192].T
    store(o_enc, genc_h)
    for c in outs:
        c.wait()


def on_device(
    teacher_in, teacher_fc1, teacher_fc2, tok_in, enc_proj, codes, ema_count, ema_sum, dec_in, head
):
    def sems(*shape):
        return pltpu.SemaphoreType.DMA(shape)

    def two(*shape):
        return [sems(*shape), sems(*shape)]

    vm = pltpu.VMEM
    local = [
        vm((ROWS, 1024), BF16), vm((4, 1024, 256), BF16), vm((4, 1024, 256), BF16),
        vm((ROWS, 192), BF16), vm((192, 32), BF16), vm((1, ROWS), jnp.int32),
        vm((HI, 128), F32), vm((HI, 128), F32), vm((32, 8192), F32), vm((32, 768), BF16),
        vm((ROWS, 1024), BF16), vm((4, ROWS, 256), BF16), vm((768, ROWS), BF16),
        vm((ROWS, 32), F32), vm((256, 256), BF16), vm((4, OWN, 256), F32),
    ]
    exchanged = [
        vm((4, 768, 256), BF16), vm((3, 4, OWN, 256), BF16), vm((32, ROWS), BF16),
        vm((3, 32, ROWS), BF16),
        vm((GRP, SROW + CROW, 128), F32), vm((GRP - 1, SROW + CROW, 128), F32),
        vm((ZED, SROW + CROW, 128), F32), vm((NMP, GRP * SROW + CROW, 128), F32),
        vm((4, OWN, 256), BF16), vm((4, OWN, 256), BF16), vm((4, OWN, 768), BF16),
        vm((GRP, GH + GX, 256), BF16), vm((GRP - 1, GH + GX, 256), BF16),
        vm((ZED, GH + GX, 256), BF16), vm((GRP, GH + GX, 256), BF16),
    ]
    results = [
        vm((HI, 128), F32), vm((32, 8192), F32), vm((768, 256), F32), vm((32, 768), F32),
        vm((192, 32), F32),
    ]
    semaphores = [sems(17), sems(5)]
    semaphores += two(3) + two(4, 3) + two(3) + two(7) + two(7) + two(7)
    semaphores += two(3) + two(3) + two(3) + two(7) + two(7) + two(7) + two(7)
    anywhere = pl.BlockSpec(memory_space=pl.ANY)
    outs = pl.pallas_call(
        kernel,
        out_shape=(
            jax.ShapeDtypeStruct((HI, 128), F32),
            jax.ShapeDtypeStruct((32, 8192), F32),
            jax.ShapeDtypeStruct((768, 256), F32),
            jax.ShapeDtypeStruct((32, 768), F32),
            jax.ShapeDtypeStruct((192, 32), F32),
        ),
        in_specs=[anywhere] * 10,
        out_specs=(anywhere,) * 5,
        scratch_shapes=local + exchanged + results + semaphores,
        compiler_params=pltpu.CompilerParams(
            collective_id=0, has_side_effects=True, vmem_limit_bytes=40 * 2**20
        ),
        name="step",
    )(
        teacher_in, teacher_fc1, teacher_fc2, tok_in, enc_proj, codes.reshape(1, ROWS),
        ema_count.reshape(HI, 128), ema_sum, dec_in, head,
    )
    return (outs[0].reshape(8192), *outs[1:])


def solution(mesh):
    placed = (
        P("dp", None),
        P(None, "mp"),
        P("mp", None),
        P("dp", "mp"),
        P("mp", None),
        P("dp"),
        P(),
        P(),
        P(),
        P(None, "mp"),
    )
    return jax.shard_map(
        on_device,
        mesh=mesh,
        in_specs=placed,
        out_specs=(P(), P(), P(None, "mp"), P(), P("mp", None)),
        check_vma=False,
    )
```

time: 1100 us -> 76.7 us (0.07)
  the two profiles are of different devices: /device:TPU:2 before, /device:TPU:1 now
where the time goes in v1:
time: 76.7 us; the launch traced here: 76.2 us
  Pallas kernels  61.3 us (80%)
  local copies, waits for them, and re-layouts  14.3 us (19%)
    pallas_call x1, Pallas kernels, on_device(): pl.pallas_call(kernel, out_shape=(jax.ShapeDtypeStruct((HI, 128), F32), j...  61.3 us
    unnamed x23, local copies, waits for them, and re-layouts  14.3 us

profile of v1, /device:TPU:1, one launch (start us, length us, event | category | flops | bytes accessed | tf_op | source)
XLA Modules:
  0.0 76.2 jit_solution(17783125285177752312)
XLA Ops:
  0.6 0.8 %copy.16.enc_h = bf16[192,32]{1,0:T(8,128)(2,1)S(1)} copy(bf16[192,32]{0,1:T(8,128)(2,1)} %param.14) | data formatting | bytes 24576 | tf_op args[4]
  1.5 1.0 %copy.15.tok_h = bf16[256,192]{1,0:T(8,128)(2,1)S(1)} copy(bf16[256,192]{0,1:T(8,128)(2,1)} %param.13) | data formatting | bytes 196608 | tf_op args[3]
  2.5 0.0 copy-start
  2.5 1.6 %copy-done = bf16[1024,1024]{1,0:T(8,128)(2,1)S(1)} copy-done((bf16[1024,1024]{1,0:T(8,128)(2,1)S(1)}, bf16[1024,1024]{1,0:T(8,128)(2,1)}, u32[]{:S(2)}) %copy-start) | copy-done | bytes 2097176
  4.1 0.0 copy-start.1
  4.1 1.6 %copy-done.1 = bf16[1024,1024]{1,0:T(8,128)(2,1)S(1)} copy-done((bf16[1024,1024]{1,0:T(8,128)(2,1)S(1)}, bf16[1024,1024]{1,0:T(8,128)(2,1)}, u32[]{:S(2)}) %copy-start.1) | copy-done | bytes 2097176
  5.7 0.0 copy-start.2
  5.7 1.2 %copy-done.2 = f32[32,8192]{1,0:T(8,128)S(1)} copy-done((f32[32,8192]{1,0:T(8,128)S(1)}, f32[32,8192]{1,0:T(8,128)}, u32[]{:S(2)}) %copy-start.2) | copy-done | bytes 1048600
  6.9 0.0 copy-start.3
  6.9 1.0 %copy-done.3 = bf16[256,1024]{1,0:T(8,128)(2,1)S(1)} copy-done((bf16[256,1024]{1,0:T(8,128)(2,1)S(1)}, bf16[256,1024]{1,0:T(8,128)(2,1)}, u32[]{:S(2)}) %copy-start.3) | copy-done | bytes 524312
  7.9 0.0 copy-start.4
  7.9 1.0 %copy-done.4 = bf16[768,256]{1,0:T(8,128)(2,1)S(1)} copy-done((bf16[768,256]{1,0:T(8,128)(2,1)S(1)}, bf16[768,256]{1,0:T(8,128)(2,1)}, u32[]{:S(2)}) %copy-start.4) | copy-done | bytes 393240
  8.9 0.0 copy-start.5
  8.9 0.8 %copy-done.5 = bf16[32,768]{1,0:T(8,128)(2,1)S(1)} copy-done((bf16[32,768]{1,0:T(8,128)(2,1)S(1)}, bf16[32,768]{1,0:T(8,128)(2,1)}, u32[]{:S(2)}) %copy-start.5) | copy-done | bytes 49176
  9.7 0.0 copy-start.6
  9.7 0.8 copy-done.6
  10.5 0.0 copy-start.7
  10.5 0.7 copy-done.7
  11.2 61.3 %step.1 = (f32[64,128]{1,0:T(8,128)S(1)}, f32[32,8192]{1,0:T(8,128)S(1)}, f32[768,256]{1,0:T(8,128)S(1)}, f32[32,768]{1,0:T(8,128)S(1)}, f32[192,32]{1,0:T(8,128)S(1)}) custom-call(bf16[256,1024]{1,0:T(8,128)(2,1)S(1)} %copy-done.3, bf16[1024,1024]{1,0:T(8,128)(2,1)S(1)} %copy-done, bf16[1024,1024]{1,0:T(8,128)(2,1)S(1)} %copy-done.1, ...), custom_call_target="tpu_custom_call" | custom-call | tf_op jit(solution)/shard_map/step/pallas_call | solution.py:438
  72.4 0.7 copy.17
  73.1 0.6 copy.22
  73.7 1.0 %copy.23 = f32[32,8192]{1,0:T(8,128)} copy(f32[32,8192]{1,0:T(8,128)S(1)} %get-tuple-element.26) | data formatting | bytes 2097152
  74.7 0.9 %copy.24 = f32[768,256]{1,0:T(8,128)} copy(f32[768,256]{1,0:T(8,128)S(1)} %get-tuple-element.27) | data formatting | bytes 1572864
  75.6 0.6 copy.25
Async XLA Ops:
  2.5 1.6 %copy-start = (bf16[1024,1024]{1,0:T(8,128)(2,1)S(1)}, bf16[1024,1024]{1,0:T(8,128)(2,1)}, u32[]{:S(2)}) copy-start(bf16[1024,1024]{1,0:T(8,128)(2,1)} %fc1_h.1) | copy-start | bytes 6291460
  4.1 1.6 %copy-start.1 = (bf16[1024,1024]{1,0:T(8,128)(2,1)S(1)}, bf16[1024,1024]{1,0:T(8,128)(2,1)}, u32[]{:S(2)}) copy-start(bf16[1024,1024]{1,0:T(8,128)(2,1)} %fc2_h.1) | copy-start | bytes 6291460
  5.7 1.2 %copy-start.2 = (f32[32,8192]{1,0:T(8,128)S(1)}, f32[32,8192]{1,0:T(8,128)}, u32[]{:S(2)}) copy-start(f32[32,8192]{1,0:T(8,128)} %sum_h.1) | copy-start | bytes 3145732
  6.9 1.0 %copy-start.3 = (bf16[256,1024]{1,0:T(8,128)(2,1)S(1)}, bf16[256,1024]{1,0:T(8,128)(2,1)}, u32[]{:S(2)}) copy-start(bf16[256,1024]{1,0:T(8,128)(2,1)} %tin_h.1) | copy-start | bytes 1572868
  7.9 1.0 %copy-start.4 = (bf16[768,256]{1,0:T(8,128)(2,1)S(1)}, bf16[768,256]{1,0:T(8,128)(2,1)}, u32[]{:S(2)}) copy-start(bf16[768,256]{1,0:T(8,128)(2,1)} %head_h.1) | copy-start | bytes 1179652
  8.9 0.8 %copy-start.5 = (bf16[32,768]{1,0:T(8,128)(2,1)S(1)}, bf16[32,768]{1,0:T(8,128)(2,1)}, u32[]{:S(2)}) copy-start(bf16[32,768]{1,0:T(8,128)(2,1)} %dec_h.1) | copy-start | bytes 147460
  9.7 0.8 copy-start.6
  10.5 0.7 copy-start.7

commit v2 on v1

--- a/solution.py
+++ b/solution.py
@@ -28,6 +28,9 @@
 CROW = 16
 GH = 96
 GX = 16
+GA = 48
+FAR = (6, 2, 5, 7, 4, 1, 3)
+FAR_Z = (4, 3, 5, 2, 6, 1, 7)
 
 
 def gelu(x):
@@ -51,7 +54,7 @@
 def kernel(
     tin_h, fc1_h, fc2_h, tok_h, enc_h, codes_h, cnt_h, sum_h, dec_h, head_h,
     ncount_h, nsum_h, ghead_h, gdec_h, genc_h,
-    tin, fc1, fc2, tok, enc, codes, cnt, inv, esum, dec,
+    tin, fc1, fc2, tok, enc, codes, cnt, esum, dec,
     th, tp, hid_t, q_rows, book, pred,
     hd, tp_r, z_s, z_r, s_s, s_r, s_z, s_all, dp_s, dp_r, dpre, g_s, g_r, g_z, g_all,
     o_count, o_sum, o_head, o_dec, o_enc,
@@ -102,52 +105,55 @@
         loads.append(c)
         return c
 
+    l_tin = load(tin_h, tin)
+    l_fc1 = [load(fc1_h.at[:, pl.ds(n * 256, 256)], fc1.at[n]) for n in range(4)]
+    l_fc2 = [load(fc2_h.at[:, pl.ds(n * 256, 256)], fc2.at[n]) for n in range(4)]
     l_tok = load(tok_h, tok)
     l_enc = load(enc_h, enc)
-    l_tin = load(tin_h, tin)
-    l_fc1 = [load(fc1_h.at[:, pl.ds(n * 256, 256)], fc1.at[n]) for n in range(4)]
     l_head = load(head_h, hd.at[mp])
-    l_fc2 = [load(fc2_h.at[:, pl.ds(n * 256, 256)], fc2.at[n]) for n in range(4)]
     l_codes = load(codes_h, codes)
     l_cnt = load(cnt_h, cnt)
     l_sum = load(sum_h, esum)
     l_dec = load(dec_h, dec)
 
-    l_tok.wait()
-    l_enc.wait()
-    z_part = dot(tok[...], enc[...])
-    z_s[...] = z_part.T.astype(BF16)
-
     l_tin.wait()
     for n in range(4):
         l_fc1[n].wait()
         th[:, n * 256:(n + 1) * 256] = gelu(dot(tin[...], fc1[n])).astype(BF16)
-
-    l_head.wait()
-    pl.semaphore_wait(barrier, len(peers))
-
-    c_z = [
-        remote(z_s, z_r.at[r - 1], z_ss.at[r - 1], z_rs.at[r - 1], mp_peer(r)) for r in (1, 2, 3)
-    ]
-    for c in c_z:
-        c.start()
-    c_wrap = remote(hd.at[mp], hd.at[mp], hd_ss.at[0], hd_rs.at[0], wrap)
-    c_wrap.start()
-    c_sib = remote(hd.at[mp], hd.at[mp], hd_ss.at[1], hd_rs.at[1], (dp, sib))
-    c_sib.start()
-
-    c_tp = []
     for n in range(4):
         l_fc2[n].wait()
         tp[n] = dot(th[...], fc2[n]).astype(BF16)
-        for r in (2, 1, 3):
-            rows = pl.ds(pl.multiple_of(lax.rem(mp + r, NMP) * OWN, OWN), OWN)
-            c = remote(
-                tp.at[n, rows], tp_r.at[r - 1, n], tp_ss.at[n, r - 1], tp_rs.at[n, r - 1],
-                mp_peer(r),
-            )
-            c.start()
-            c_tp.append(c)
+
+    l_tok.wait()
+    l_enc.wait()
+    z_s[...] = dot(enc[...], tok[...]).astype(BF16)
+    l_head.wait()
+
+    pl.semaphore_wait(barrier, len(peers))
+    c_z = [
+        remote(z_s, z_r.at[r - 1], z_ss.at[r - 1], z_rs.at[r - 1], mp_peer(r)) for r in (2, 1, 3)
+    ]
+    for c in c_z:
+        c.start()
+    cuts = (pl.ds(0, 320), pl.ds(320, 320), pl.ds(640, 128))
+    c_wrap = []
+    for i, dev in enumerate((wrap, wrap, (dp, over))):
+        c_wrap.append(
+            remote(hd.at[mp, cuts[i]], hd.at[mp, cuts[i]], hd_ss.at[i], hd_rs.at[i], dev)
+        )
+    c_wrap[0].start()
+    c_tp = []
+    for r in (2, 1, 3):
+        rows = pl.ds(pl.multiple_of(lax.rem(mp + r, NMP) * OWN, OWN), OWN)
+        c = remote(
+            tp.at[:, rows], tp_r.at[r - 1], tp_ss.at[r - 1], tp_rs.at[r - 1], mp_peer(r)
+        )
+        c.start()
+        c_tp.append(c)
+    c_wrap[1].start()
+    c_wrap[2].start()
+    c_sib = remote(hd.at[mp], hd.at[mp], hd_ss.at[3], hd_rs.at[3], (dp, sib))
+    c_sib.start()
 
     l_codes.wait()
     l_cnt.wait()
@@ -158,23 +164,23 @@
     code_lo = jnp.broadcast_to(jnp.bitwise_and(codes[...], 127), (128, ROWS))
     lo_id = lax.broadcasted_iota(jnp.int32, (128, ROWS), 0)
     lo_hot = jnp.where(lo_id == code_lo, 1.0, 0.0).astype(BF16)
-    inv[...] = 1.0 / cnt[...]
-
-    def look(i, total):
+    lo_twice = jnp.concatenate([lo_hot, lo_hot], axis=0)
+    inv = 1.0 / cnt[...]
+    for h in range(HI):
+        part = esum[:, h * 128:(h + 1) * 128] * inv[h:h + 1, :]
+        upper = part.astype(BF16)
+        book[h * 32:(h + 1) * 32, 0:128] = upper
+        book[h * 32:(h + 1) * 32, 128:256] = (part - upper.astype(F32)).astype(BF16)
+    q_t = jnp.zeros((32, ROWS), F32)
+    for i in range(HI // 8):
+        found = dot(book[i * 256:(i + 1) * 256, :], lo_twice)
         for j in range(8):
-            h = i * 8 + j
-            part = esum[:, pl.ds(pl.multiple_of(h * 128, 128), 128)] * inv[pl.ds(h, 1), :]
-            upper = part.astype(BF16)
-            book[j * 32:(j + 1) * 32, 0:128] = upper
-            book[j * 32:(j + 1) * 32, 128:256] = (part - upper.astype(F32)).astype(BF16)
-        found = dot(book[...], jnp.concatenate([lo_hot, lo_hot], axis=0))
-        for j in range(8):
-            total = total + jnp.where(code_hi == i * 8 + j, found[j * 32:(j + 1) * 32], 0.0)
-        return total
-
-    q_t = lax.fori_loop(0, HI // 8, look, jnp.zeros((32, ROWS), F32))
+            q_t = q_t + jnp.where(code_hi == i * 8 + j, found[j * 32:(j + 1) * 32], 0.0)
     q_rows[...] = q_t.T
     q_round_t = q_t.astype(BF16)
+    own_rows = pl.ds(pl.multiple_of(mp * OWN, OWN), OWN)
+    hidden, slope = gelu_and_slope(dot(q_rows[own_rows, :].astype(BF16), dec[...]))
+    hidden = hidden.astype(BF16)
 
     for c in c_z:
         c.wait()
@@ -196,29 +202,28 @@
     for i in range(GRP):
         s_s[i, SROW:SROW + CROW] = counts
     c_s1 = []
-    for k in (6, 2, 5, 7, 4, 1, 3):
+    for k in FAR:
         c = remote(
             s_s.at[grp_index(k)], s_r.at[k - 1], s1_ss.at[k - 1], s1_rs.at[k - 1], grp_peer(k)
         )
         c.start()
         c_s1.append(c)
 
-    dec_t = dec[...].astype(F32).T.astype(BF16)
-    for n in range(3):
-        hid_t[n * 256:(n + 1) * 256, :] = gelu(
-            dot(dec_t[n * 256:(n + 1) * 256], q_round_t)
-        ).astype(BF16)
-    own_rows = pl.ds(pl.multiple_of(mp * OWN, OWN), OWN)
-    hidden, slope = gelu_and_slope(dot(q_rows[own_rows, :].astype(BF16), dec[...]))
-    hidden = hidden.astype(BF16)
-
-    c_wrap.wait()
-    c_fwd = remote(hd.at[over], hd.at[over], hd_ss.at[2], hd_rs.at[2], (dp, sib))
-    c_fwd.start()
     c_sib.wait()
+    c_fwd = []
+    for i in range(2):
+        c_wrap[i].wait()
+        c = remote(hd.at[over, cuts[i]], hd.at[over, cuts[i]], hd_ss.at[4 + i], hd_rs.at[4 + i], (dp, sib))
+        c.start()
+        c_fwd.append(c)
+    c_wrap[2].wait()
+    c = remote(hd.at[over, cuts[2]], hd.at[over, cuts[2]], hd_ss.at[6], hd_rs.at[6], (dp, sib))
+    c.start()
+    c_fwd.append(c)
     for b in (mp, sib, over):
         pred[b] = dot(hidden, hd[b])
-    c_fwd.wait()
+    for c in c_fwd:
+        c.wait()
     pred[sib_over] = dot(hidden, hd[sib_over])
 
     for c in c_tp:
@@ -262,6 +267,27 @@
         c.start()
         c_dr.append(c)
 
+    dec_t = dec[...].astype(F32).T.astype(BF16)
+    for n in range(3):
+        hid_t[n * 256:(n + 1) * 256, :] = gelu(
+            dot(dec_t[n * 256:(n + 1) * 256], q_round_t)
+        ).astype(BF16)
+
+    for c in c_dp:
+        c.wait()
+    grad = dot(hid_t[...], dp_r[...].reshape(ROWS, 256)).astype(BF16)
+    for i in range(GRP):
+        g_s[i, 0:GH] = grad[i * GH:(i + 1) * GH]
+    c_g1 = [[], []]
+    for part, rows in enumerate((pl.ds(0, GA), pl.ds(GA, GH - GA))):
+        for k in FAR:
+            c = remote(
+                g_s.at[grp_index(k), rows], g_r.at[k - 1, rows],
+                g1_ss.at[part, k - 1], g1_rs.at[part, k - 1], grp_peer(k),
+            )
+            c.start()
+            c_g1[part].append(c)
+
     for c in c_s1:
         c.wait()
     s_part = s_s[grp]
@@ -269,24 +295,10 @@
         s_part = s_part + s_r[k]
     s_z[zed] = s_part
     c_s2 = []
-    for k in (4, 3, 5, 2, 6, 1, 7):
+    for k in FAR_Z:
         c = remote(s_z.at[zed], s_z.at[zed], s2_ss.at[k - 1], s2_rs.at[k - 1], zed_peer(k))
         c.start()
         c_s2.append(c)
-
-    for c in c_dp:
-        c.wait()
-    grad = dot(hid_t[...], dp_r[...].reshape(ROWS, 256)).astype(BF16)
-    for i in range(GRP):
-        g_s[i, 0:GH] = grad[i * GH:(i + 1) * GH]
-    c_g1 = []
-    for k in (6, 2, 5, 7, 4, 1, 3):
-        c = remote(
-            g_s.at[grp_index(k), pl.ds(0, GH)], g_r.at[k - 1, pl.ds(0, GH)],
-            g1_ss.at[k - 1], g1_rs.at[k - 1], grp_peer(k),
-        )
-        c.start()
-        c_g1.append(c)
 
     for c in c_dr:
         c.wait()
@@ -294,7 +306,7 @@
     dq_t = dot(dec[...], dpre_all, 1, 1)
     dz_t = (dq_t + 2.0 * BETA * (z_t - q_t)).astype(BF16)
     grad_dec = dot(q_round_t, dpre_all).astype(BF16)
-    grad_enc = dot(dz_t, tok[...]).astype(BF16)
+    grad_enc = dot(dz_t, tok[...], 1, 1).astype(BF16)
     for n in range(3):
         for i in range(2):
             g_s[n * 2 + i, GH:GH + GX] = grad_dec[i * 16:(i + 1) * 16, n * 256:(n + 1) * 256]
@@ -302,13 +314,28 @@
         g_s[6 + i, GH:GH + GX, 0:192] = grad_enc[i * 16:(i + 1) * 16]
         g_s[6 + i, GH:GH + GX, 192:256] = jnp.zeros((GX, 64), BF16)
     c_x1 = []
-    for k in (6, 2, 5, 7, 4, 1, 3):
+    for k in FAR:
         c = remote(
             g_s.at[grp_index(k), pl.ds(GH, GX)], g_r.at[k - 1, pl.ds(GH, GX)],
             x1_ss.at[k - 1], x1_rs.at[k - 1], grp_peer(k),
         )
         c.start()
         c_x1.append(c)
+
+    halves = ((0, GA), (GA, GH + GX - GA))
+    c_g2 = [[], []]
+    for part, (first, size) in enumerate(halves):
+        for c in c_g1[part] + (c_x1 if part == 1 else []):
+            c.wait()
+        g_part = g_s[grp, first:first + size].astype(F32)
+        for k in range(GRP - 1):
+            g_part = g_part + g_r[k, first:first + size].astype(F32)
+        g_z[zed, first:first + size] = g_part.astype(BF16)
+        for k in FAR_Z:
+            rows = g_z.at[zed, pl.ds(first, size)]
+            c = remote(rows, rows, g2_ss.at[part, k - 1], g2_rs.at[part, k - 1], zed_peer(k))
+            c.start()
+            c_g2[part].append(c)
 
     for c in c_s2:
         c.wait()
@@ -319,7 +346,7 @@
     s_all[mp, own_part] = s_part[0:SROW]
     s_all[mp, pl.ds(GRP * SROW, CROW)] = s_part[SROW:SROW + CROW]
     c_s3 = []
-    for k in (6, 2, 5, 7, 4, 1, 3):
+    for k in FAR:
         c = remote(
             s_all.at[mp, own_part], s_all.at[mp, own_part], s3_ss.at[k - 1], s3_rs.at[k - 1],
             grp_peer(k),
@@ -327,17 +354,19 @@
         c.start()
         c_s3.append(c)
 
-    for c in c_g1 + c_x1:
-        c.wait()
-    g_part = g_s[grp].astype(F32)
-    for k in range(GRP - 1):
-        g_part = g_part + g_r[k].astype(F32)
-    g_z[zed] = g_part.astype(BF16)
-    c_g2 = []
-    for k in (4, 3, 5, 2, 6, 1, 7):
-        c = remote(g_z.at[zed], g_z.at[zed], g2_ss.at[k - 1], g2_rs.at[k - 1], zed_peer(k))
-        c.start()
-        c_g2.append(c)
+    c_g3 = [[], []]
+    for part, (first, size) in enumerate(halves):
+        for c in c_g2[part]:
+            c.wait()
+        g_part = g_z[0, first:first + size].astype(F32)
+        for k in range(1, ZED):
+            g_part = g_part + g_z[k, first:first + size].astype(F32)
+        g_all[grp, first:first + size] = g_part.astype(BF16)
+        for k in FAR:
+            rows = g_all.at[grp, pl.ds(first, size)]
+            c = remote(rows, rows, g3_ss.at[part, k - 1], g3_rs.at[part, k - 1], grp_peer(k))
+            c.start()
+            c_g3[part].append(c)
 
     for c in c_s3:
         c.wait()
@@ -349,55 +378,52 @@
     c_last = remote(s_all.at[over], s_all.at[over], s4_ss.at[2], s4_rs.at[2], (dp, sib))
     c_last.start()
 
-    for c in c_g2:
-        c.wait()
-    g_part = g_z[0].astype(F32)
-    for k in range(1, ZED):
-        g_part = g_part + g_z[k].astype(F32)
-    g_all[grp] = g_part.astype(BF16)
-    c_g3 = []
-    for k in (6, 2, 5, 7, 4, 1, 3):
-        c = remote(g_all.at[grp], g_all.at[grp], g3_ss.at[k - 1], g3_rs.at[k - 1], grp_peer(k))
-        c.start()
-        c_g3.append(c)
-
     c_near.wait()
     c_last.wait()
+    outs = []
+
+    def store(src, dst):
+        c = pltpu.make_async_copy(src, dst, out_sem.at[len(outs)])
+        c.start()
+        outs.append(c)
+
     for m in range(NMP):
-        o_count[m * CROW:(m + 1) * CROW] = s_all[m, GRP * SROW:GRP * SROW + CROW]
+        o_count[m * CROW:(m + 1) * CROW] = (
+            DECAY * cnt[m * CROW:(m + 1) * CROW]
+            + (1.0 - DECAY) * s_all[m, GRP * SROW:GRP * SROW + CROW]
+        )
         for i in range(QHI):
             columns = slice((m * QHI + i) * 128, (m * QHI + i + 1) * 128)
             o_sum[:, columns] = DECAY * esum[:, columns] + (1.0 - DECAY) * s_all[
                 m, i * 32:(i + 1) * 32
             ]
-    o_count[...] = DECAY * cnt[...] + (1.0 - DECAY) * o_count[...]
-    outs = []
-
-    def store(src, dst):
-        c = pltpu.make_async_copy(src, dst, out_sem.at[len(outs)])
-        c.start()
-        outs.append(c)
-
     store(o_count, ncount_h)
     store(o_sum, nsum_h)
 
-    for c in c_g3:
-        c.wait()
-    for i in range(GRP):
-        o_head[i * GH:(i + 1) * GH] = g_all[i, 0:GH].astype(F32)
-    store(o_head, ghead_h)
+    for part, rows in enumerate((slice(0, GA), slice(GA, GH))):
+        for c in c_g3[part]:
+            c.wait()
+        for i in range(GRP):
+            o_head[i, rows] = g_all[i, rows].astype(F32)
+        store(o_head.at[:, rows], ghead_h.at[:, rows])
     for n in range(3):
         for i in range(2):
             o_dec[i * 16:(i + 1) * 16, n * 256:(n + 1) * 256] = g_all[
                 n * 2 + i, GH:GH + GX
             ].astype(F32)
     store(o_dec, gdec_h)
-    enc_t = jnp.concatenate(
-        [g_all[6, GH:GH + GX].astype(F32), g_all[7, GH:GH + GX].astype(F32)], axis=0
-    )
-    o_enc[...] = enc_t[:, 0:192].T
+    for i in range(2):
+        o_enc[i * 16:(i + 1) * 16] = g_all[6 + i, GH:GH + GX, 0:192].astype(F32)
     store(o_enc, genc_h)
     for c in outs:
+        c.wait()
+
+
+def copy_out(*refs):
+    copies = [pltpu.make_async_copy(refs[i], refs[5 + i], refs[10].at[i]) for i in range(5)]
+    for c in copies:
+        c.start()
+    for c in copies:
         c.wait()
 
 
@@ -413,10 +439,10 @@
     vm = pltpu.VMEM
     local = [
         vm((ROWS, 1024), BF16), vm((4, 1024, 256), BF16), vm((4, 1024, 256), BF16),
-        vm((ROWS, 192), BF16), vm((192, 32), BF16), vm((1, ROWS), jnp.int32),
-        vm((HI, 128), F32), vm((HI, 128), F32), vm((32, 8192), F32), vm((32, 768), BF16),
+        vm((192, ROWS), BF16), vm((32, 192), BF16), vm((1, ROWS), jnp.int32),
+        vm((HI, 128), F32), vm((32, 8192), F32), vm((32, 768), BF16),
         vm((ROWS, 1024), BF16), vm((4, ROWS, 256), BF16), vm((768, ROWS), BF16),
-        vm((ROWS, 32), F32), vm((256, 256), BF16), vm((4, OWN, 256), F32),
+        vm((ROWS, 32), F32), vm((HI * 32, 256), BF16), vm((4, OWN, 256), F32),
     ]
     exchanged = [
         vm((4, 768, 256), BF16), vm((3, 4, OWN, 256), BF16), vm((32, ROWS), BF16),
@@ -428,34 +454,43 @@
         vm((ZED, GH + GX, 256), BF16), vm((GRP, GH + GX, 256), BF16),
     ]
     results = [
-        vm((HI, 128), F32), vm((32, 8192), F32), vm((768, 256), F32), vm((32, 768), F32),
-        vm((192, 32), F32),
+        vm((HI, 128), F32), vm((32, 8192), F32), vm((GRP, GH, 256), F32), vm((32, 768), F32),
+        vm((32, 192), F32),
     ]
-    semaphores = [sems(17), sems(5)]
-    semaphores += two(3) + two(4, 3) + two(3) + two(7) + two(7) + two(7)
-    semaphores += two(3) + two(3) + two(3) + two(7) + two(7) + two(7) + two(7)
+    semaphores = [sems(16), sems(6)]
+    semaphores += two(7) + two(3) + two(3) + two(7) + two(7) + two(7)
+    semaphores += two(3) + two(3) + two(3) + two(2, 7) + two(7) + two(2, 7) + two(2, 7)
     anywhere = pl.BlockSpec(memory_space=pl.ANY)
     outs = pl.pallas_call(
         kernel,
         out_shape=(
             jax.ShapeDtypeStruct((HI, 128), F32),
             jax.ShapeDtypeStruct((32, 8192), F32),
-            jax.ShapeDtypeStruct((768, 256), F32),
+            jax.ShapeDtypeStruct((GRP, GH, 256), F32),
             jax.ShapeDtypeStruct((32, 768), F32),
-            jax.ShapeDtypeStruct((192, 32), F32),
+            jax.ShapeDtypeStruct((32, 192), F32),
         ),
-        in_specs=[anywhere] * 10,
+        in_specs=[pl.BlockSpec(memory_space=pltpu.HBM)] * 10,
         out_specs=(anywhere,) * 5,
         scratch_shapes=local + exchanged + results + semaphores,
         compiler_params=pltpu.CompilerParams(
-            collective_id=0, has_side_effects=True, vmem_limit_bytes=40 * 2**20
+            collective_id=0, has_side_effects=True, vmem_limit_bytes=64 * 2**20
         ),
         name="step",
     )(
-        teacher_in, teacher_fc1, teacher_fc2, tok_in, enc_proj, codes.reshape(1, ROWS),
+        teacher_in, teacher_fc1, teacher_fc2, tok_in.T, enc_proj.T, codes.reshape(1, ROWS),
         ema_count.reshape(HI, 128), ema_sum, dec_in, head,
     )
-    return (outs[0].reshape(8192), *outs[1:])
+    outs = pl.pallas_call(
+        copy_out,
+        out_shape=tuple(jax.ShapeDtypeStruct(o.shape, o.dtype) for o in outs),
+        in_specs=[anywhere] * 5,
+        out_specs=(pl.BlockSpec(memory_space=pltpu.HBM),) * 5,
+        scratch_shapes=[sems(5)],
+        compiler_params=pltpu.CompilerParams(vmem_limit_bytes=64 * 2**20),
+        name="results",
+    )(*outs)
+    return (outs[0].reshape(8192), outs[1], outs[2].reshape(768, 256), outs[3], outs[4].T)
 
 
 def solution(mesh):

time: 76.7 us -> 125 us (1.63)
  Pallas kernels: 61.3 us -> 124 us
  local copies, waits for them, and re-layouts: 14.3 us -> 0 us
    pallas_call x0 -> x1, Pallas kernels: none -> 61.7 us  [on_device(): pl.pallas_call(copy_out, out_shape=tuple((jax.ShapeDtypeStruct(o.shape, o...]
    unnamed x23 -> x0, local copies, waits for them, and re-layouts: 14.3 us -> none
where the time goes in v2:
time: 125 us
  Pallas kernels  124 us (99%)
    pallas_call x1, Pallas kernels, on_device(): pl.pallas_call(kernel, out_shape=(jax.ShapeDtypeStruct((HI, 128), F32), j...  62.3 us
    pallas_call x1, Pallas kernels, on_device(): pl.pallas_call(copy_out, out_shape=tuple((jax.ShapeDtypeStruct(o.shape, o...  61.7 us

profile of v2, /device:TPU:1, one launch (start us, length us, event | category | flops | bytes accessed | tf_op | source)
XLA Modules:
  0.0 124.7 jit_solution(10071407629747095742)
XLA Ops:
  0.6 62.3 %step.1 = (f32[64,128]{1,0:T(8,128)}, f32[32,8192]{1,0:T(8,128)}, f32[8,96,256]{2,1,0:T(8,128)}, f32[32,768]{1,0:T(8,128)}, f32[32,192]{1,0:T(8,128)}) custom-call(bf16[256,1024]{1,0:T(8,128)(2,1)} %tin_h.1, bf16[1024,1024]{1,0:T(8,128)(2,1)} %fc1_h.1, bf16[1024,1024]{1,0:T(8,128)(2,1)} %fc2_h.1, bf16[192,256]{1,0:T(8,128)(2,1)} %bitcast.7, ...), custom_call_target="tpu_custom_call" | custom-call | tf_op jit(solution)/shard_map/step/pallas_call | solution.py:464
  63.0 61.7 %results.1 = (f32[64,128]{1,0:T(8,128)}, f32[32,8192]{1,0:T(8,128)}, f32[8,96,256]{2,1,0:T(8,128)}, f32[32,768]{1,0:T(8,128)}, f32[32,192]{1,0:T(8,128)}) custom-call(f32[64,128]{1,0:T(8,128)} %get-tuple-element.15.refs_0_, f32[32,8192]{1,0:T(8,128)} %get-tuple-element.16.refs_1_, f32[8,96,256]{2,1,0:T(8,128)} %get-tuple-element.17.refs_2_, ...), custom_call_target="tpu_custom_call" | custom-call | tf_op jit(solution)/shard_map/results/pallas_call | solution.py:484

commit v3 on v2

--- a/solution.py
+++ b/solution.py
@@ -29,6 +29,7 @@
 GH = 96
 GX = 16
 GA = 48
+SPLIT = 264
 FAR = (6, 2, 5, 7, 4, 1, 3)
 FAR_Z = (4, 3, 5, 2, 6, 1, 7)
 
@@ -106,11 +107,11 @@
         return c
 
     l_tin = load(tin_h, tin)
-    l_fc1 = [load(fc1_h.at[:, pl.ds(n * 256, 256)], fc1.at[n]) for n in range(4)]
-    l_fc2 = [load(fc2_h.at[:, pl.ds(n * 256, 256)], fc2.at[n]) for n in range(4)]
     l_tok = load(tok_h, tok)
     l_enc = load(enc_h, enc)
+    l_fc1 = [load(fc1_h.at[:, pl.ds(n * 256, 256)], fc1.at[n]) for n in range(4)]
     l_head = load(head_h, hd.at[mp])
+    l_fc2 = [load(fc2_h.at[:, pl.ds(n * 256, 256)], fc2.at[n]) for n in range(4)]
     l_codes = load(codes_h, codes)
     l_cnt = load(cnt_h, cnt)
     l_sum = load(sum_h, esum)
@@ -120,9 +121,6 @@
     for n in range(4):
         l_fc1[n].wait()
         th[:, n * 256:(n + 1) * 256] = gelu(dot(tin[...], fc1[n])).astype(BF16)
-    for n in range(4):
-        l_fc2[n].wait()
-        tp[n] = dot(th[...], fc2[n]).astype(BF16)
 
     l_tok.wait()
     l_enc.wait()
@@ -141,7 +139,14 @@
         c_wrap.append(
             remote(hd.at[mp, cuts[i]], hd.at[mp, cuts[i]], hd_ss.at[i], hd_rs.at[i], dev)
         )
-    c_wrap[0].start()
+    for c in c_wrap:
+        c.start()
+    c_sib = remote(hd.at[mp], hd.at[mp], hd_ss.at[3], hd_rs.at[3], (dp, sib))
+    c_sib.start()
+
+    for n in range(4):
+        l_fc2[n].wait()
+        tp[n] = dot(th[...], fc2[n]).astype(BF16)
     c_tp = []
     for r in (2, 1, 3):
         rows = pl.ds(pl.multiple_of(lax.rem(mp + r, NMP) * OWN, OWN), OWN)
@@ -150,37 +155,13 @@
         )
         c.start()
         c_tp.append(c)
-    c_wrap[1].start()
-    c_wrap[2].start()
-    c_sib = remote(hd.at[mp], hd.at[mp], hd_ss.at[3], hd_rs.at[3], (dp, sib))
-    c_sib.start()
 
     l_codes.wait()
-    l_cnt.wait()
-    l_sum.wait()
-    l_dec.wait()
     code = jnp.broadcast_to(codes[...], (32, ROWS))
     code_hi = jnp.right_shift(code, 7)
     code_lo = jnp.broadcast_to(jnp.bitwise_and(codes[...], 127), (128, ROWS))
     lo_id = lax.broadcasted_iota(jnp.int32, (128, ROWS), 0)
     lo_hot = jnp.where(lo_id == code_lo, 1.0, 0.0).astype(BF16)
-    lo_twice = jnp.concatenate([lo_hot, lo_hot], axis=0)
-    inv = 1.0 / cnt[...]
-    for h in range(HI):
-        part = esum[:, h * 128:(h + 1) * 128] * inv[h:h + 1, :]
-        upper = part.astype(BF16)
-        book[h * 32:(h + 1) * 32, 0:128] = upper
-        book[h * 32:(h + 1) * 32, 128:256] = (part - upper.astype(F32)).astype(BF16)
-    q_t = jnp.zeros((32, ROWS), F32)
-    for i in range(HI // 8):
-        found = dot(book[i * 256:(i + 1) * 256, :], lo_twice)
-        for j in range(8):
-            q_t = q_t + jnp.where(code_hi == i * 8 + j, found[j * 32:(j + 1) * 32], 0.0)
-    q_rows[...] = q_t.T
-    q_round_t = q_t.astype(BF16)
-    own_rows = pl.ds(pl.multiple_of(mp * OWN, OWN), OWN)
-    hidden, slope = gelu_and_slope(dot(q_rows[own_rows, :].astype(BF16), dec[...]))
-    hidden = hidden.astype(BF16)
 
     for c in c_z:
         c.wait()
@@ -209,17 +190,35 @@
         c.start()
         c_s1.append(c)
 
+    l_cnt.wait()
+    l_sum.wait()
+    l_dec.wait()
+    lo_twice = jnp.concatenate([lo_hot, lo_hot], axis=0)
+    inv = 1.0 / cnt[...]
+    for h in range(HI):
+        part = esum[:, h * 128:(h + 1) * 128] * inv[h:h + 1, :]
+        upper = part.astype(BF16)
+        book[h * 32:(h + 1) * 32, 0:128] = upper
+        book[h * 32:(h + 1) * 32, 128:256] = (part - upper.astype(F32)).astype(BF16)
+    q_t = jnp.zeros((32, ROWS), F32)
+    for i in range(HI // 8):
+        found = dot(book[i * 256:(i + 1) * 256, :], lo_twice)
+        for j in range(8):
+            q_t = q_t + jnp.where(code_hi == i * 8 + j, found[j * 32:(j + 1) * 32], 0.0)
+    q_rows[...] = q_t.T
+    q_round_t = q_t.astype(BF16)
+    own_rows = pl.ds(pl.multiple_of(mp * OWN, OWN), OWN)
+    hidden, slope = gelu_and_slope(dot(q_rows[own_rows, :].astype(BF16), dec[...]))
+    hidden = hidden.astype(BF16)
+
     c_sib.wait()
     c_fwd = []
-    for i in range(2):
+    for i in range(3):
         c_wrap[i].wait()
-        c = remote(hd.at[over, cuts[i]], hd.at[over, cuts[i]], hd_ss.at[4 + i], hd_rs.at[4 + i], (dp, sib))
+        rows = hd.at[over, cuts[i]]
+        c = remote(rows, rows, hd_ss.at[4 + i], hd_rs.at[4 + i], (dp, sib))
         c.start()
         c_fwd.append(c)
-    c_wrap[2].wait()
-    c = remote(hd.at[over, cuts[2]], hd.at[over, cuts[2]], hd_ss.at[6], hd_rs.at[6], (dp, sib))
-    c.start()
-    c_fwd.append(c)
     for b in (mp, sib, over):
         pred[b] = dot(hidden, hd[b])
     for c in c_fwd:
@@ -267,6 +266,18 @@
         c.start()
         c_dr.append(c)
 
+    for c in c_s1:
+        c.wait()
+    s_part = s_s[grp]
+    for k in range(GRP - 1):
+        s_part = s_part + s_r[k]
+    s_z[zed] = s_part
+    c_s2 = []
+    for k in FAR_Z:
+        c = remote(s_z.at[zed], s_z.at[zed], s2_ss.at[k - 1], s2_rs.at[k - 1], zed_peer(k))
+        c.start()
+        c_s2.append(c)
+
     dec_t = dec[...].astype(F32).T.astype(BF16)
     for n in range(3):
         hid_t[n * 256:(n + 1) * 256, :] = gelu(
@@ -287,18 +298,6 @@
             )
             c.start()
             c_g1[part].append(c)
-
-    for c in c_s1:
-        c.wait()
-    s_part = s_s[grp]
-    for k in range(GRP - 1):
-        s_part = s_part + s_r[k]
-    s_z[zed] = s_part
-    c_s2 = []
-    for k in FAR_Z:
-        c = remote(s_z.at[zed], s_z.at[zed], s2_ss.at[k - 1], s2_rs.at[k - 1], zed_peer(k))
-        c.start()
-        c_s2.append(c)
 
     for c in c_dr:
         c.wait()
@@ -324,9 +323,10 @@
 
     halves = ((0, GA), (GA, GH + GX - GA))
     c_g2 = [[], []]
-    for part, (first, size) in enumerate(halves):
-        for c in c_g1[part] + (c_x1 if part == 1 else []):
-            c.wait()
+    c_g3 = [[], []]
+
+    def along_z(part):
+        first, size = halves[part]
         g_part = g_s[grp, first:first + size].astype(F32)
         for k in range(GRP - 1):
             g_part = g_part + g_r[k, first:first + size].astype(F32)
@@ -336,6 +336,24 @@
             c = remote(rows, rows, g2_ss.at[part, k - 1], g2_rs.at[part, k - 1], zed_peer(k))
             c.start()
             c_g2[part].append(c)
+
+    def gather(part):
+        first, size = halves[part]
+        for c in c_g2[part]:
+            c.wait()
+        g_part = g_z[0, first:first + size].astype(F32)
+        for k in range(1, ZED):
+            g_part = g_part + g_z[k, first:first + size].astype(F32)
+        g_all[grp, first:first + size] = g_part.astype(BF16)
+        for k in FAR:
+            rows = g_all.at[grp, pl.ds(first, size)]
+            c = remote(rows, rows, g3_ss.at[part, k - 1], g3_rs.at[part, k - 1], grp_peer(k))
+            c.start()
+            c_g3[part].append(c)
+
+    for c in c_g1[0]:
+        c.wait()
+    along_z(0)
 
     for c in c_s2:
         c.wait()
@@ -354,32 +372,34 @@
         c.start()
         c_s3.append(c)
 
-    c_g3 = [[], []]
-    for part, (first, size) in enumerate(halves):
-        for c in c_g2[part]:
-            c.wait()
-        g_part = g_z[0, first:first + size].astype(F32)
-        for k in range(1, ZED):
-            g_part = g_part + g_z[k, first:first + size].astype(F32)
-        g_all[grp, first:first + size] = g_part.astype(BF16)
-        for k in FAR:
-            rows = g_all.at[grp, pl.ds(first, size)]
-            c = remote(rows, rows, g3_ss.at[part, k - 1], g3_rs.at[part, k - 1], grp_peer(k))
-            c.start()
-            c_g3[part].append(c)
+    for c in c_g1[1] + c_x1:
+        c.wait()
+    along_z(1)
+    gather(0)
 
     for c in c_s3:
         c.wait()
-    c_over = remote(s_all.at[mp], s_all.at[mp], s4_ss.at[0], s4_rs.at[0], (dp, over))
-    c_over.start()
-    c_near = remote(s_all.at[mp], s_all.at[mp], s4_ss.at[1], s4_rs.at[1], (dp, sib))
+    parts = (pl.ds(0, SPLIT), pl.ds(SPLIT, GRP * SROW + CROW - SPLIT))
+    c_over = []
+    for i, dev in enumerate(((dp, over), wrap)):
+        rows = s_all.at[mp, parts[i]]
+        c = remote(rows, rows, s4_ss.at[i], s4_rs.at[i], dev)
+        c.start()
+        c_over.append(c)
+    c_near = remote(s_all.at[mp], s_all.at[mp], s4_ss.at[2], s4_rs.at[2], (dp, sib))
     c_near.start()
-    c_over.wait()
-    c_last = remote(s_all.at[over], s_all.at[over], s4_ss.at[2], s4_rs.at[2], (dp, sib))
-    c_last.start()
-
-    c_near.wait()
-    c_last.wait()
+
+    gather(1)
+    c_last = []
+    for i in range(2):
+        c_over[i].wait()
+        rows = s_all.at[over, parts[i]]
+        c = remote(rows, rows, s4_ss.at[3 + i], s4_rs.at[3 + i], (dp, sib))
+        c.start()
+        c_last.append(c)
+
+    for c in c_last + [c_near]:
+        c.wait()
     outs = []
 
     def store(src, dst):
@@ -420,10 +440,22 @@
 
 
 def copy_out(*refs):
-    copies = [pltpu.make_async_copy(refs[i], refs[5 + i], refs[10].at[i]) for i in range(5)]
-    for c in copies:
-        c.start()
-    for c in copies:
+    arrays, results, buffers, (in_sem, out_sem) = refs[0:5], refs[5:10], refs[10:15], refs[15:]
+    pieces = [(1, (slice(None), pl.ds(i * 2048, 2048))) for i in range(4)]
+    pieces += [(2, (pl.ds(i * 2, 2),)) for i in range(4)]
+    pieces += [(i, (slice(None),)) for i in (0, 3, 4)]
+    ins = []
+    for i, (a, at) in enumerate(pieces):
+        c = pltpu.make_async_copy(arrays[a].at[at], buffers[a].at[at], in_sem.at[i])
+        c.start()
+        ins.append(c)
+    outs = []
+    for i, (a, at) in enumerate(pieces):
+        ins[i].wait()
+        c = pltpu.make_async_copy(buffers[a].at[at], results[a].at[at], out_sem.at[i])
+        c.start()
+        outs.append(c)
+    for c in outs:
         c.wait()
 
 
@@ -459,7 +491,7 @@
     ]
     semaphores = [sems(16), sems(6)]
     semaphores += two(7) + two(3) + two(3) + two(7) + two(7) + two(7)
-    semaphores += two(3) + two(3) + two(3) + two(2, 7) + two(7) + two(2, 7) + two(2, 7)
+    semaphores += two(5) + two(3) + two(3) + two(2, 7) + two(7) + two(2, 7) + two(2, 7)
     anywhere = pl.BlockSpec(memory_space=pl.ANY)
     outs = pl.pallas_call(
         kernel,
@@ -484,9 +516,9 @@
     outs = pl.pallas_call(
         copy_out,
         out_shape=tuple(jax.ShapeDtypeStruct(o.shape, o.dtype) for o in outs),
-        in_specs=[anywhere] * 5,
+        in_specs=[pl.BlockSpec(memory_space=pltpu.HBM)] * 5,
         out_specs=(pl.BlockSpec(memory_space=pltpu.HBM),) * 5,
-        scratch_shapes=[sems(5)],
+        scratch_shapes=[vm(o.shape, o.dtype) for o in outs] + two(11),
         compiler_params=pltpu.CompilerParams(vmem_limit_bytes=64 * 2**20),
         name="results",
     )(*outs)

time: 125 us -> 55.5 us (0.44)
  Pallas kernels: 124 us -> 54.7 us
    pallas_call x1, Pallas kernels: 61.7 us -> 2.4 us  [on_device(): pl.pallas_call(copy_out, out_shape=tuple((jax.ShapeDtypeStruct(o.shape, o...]
    pallas_call x1, Pallas kernels: 62.3 us -> 52.3 us  [on_device(): pl.pallas_call(kernel, out_shape=(jax.ShapeDtypeStruct((HI, 128), F32), j...]
where the time goes in v3:
time: 55.5 us; the launch traced here: 55.3 us
  Pallas kernels  54.7 us (99%)
  between operations  0.64 us (1%)
    pallas_call x1, Pallas kernels, on_device(): pl.pallas_call(kernel, out_shape=(jax.ShapeDtypeStruct((HI, 128), F32), j...  52.3 us
    pallas_call x1, Pallas kernels, on_device(): pl.pallas_call(copy_out, out_shape=tuple((jax.ShapeDtypeStruct(o.shape, o...  2.4 us

profile of v3, /device:TPU:1, one launch (start us, length us, event | category | flops | bytes accessed | tf_op | source)
XLA Modules:
  0.0 55.3 jit_solution(11008196813378725224)
XLA Ops:
  0.6 52.3 %step.1 = (f32[64,128]{1,0:T(8,128)}, f32[32,8192]{1,0:T(8,128)}, f32[8,96,256]{2,1,0:T(8,128)}, f32[32,768]{1,0:T(8,128)}, f32[32,192]{1,0:T(8,128)}) custom-call(bf16[256,1024]{1,0:T(8,128)(2,1)} %tin_h.1, bf16[1024,1024]{1,0:T(8,128)(2,1)} %fc1_h.1, bf16[1024,1024]{1,0:T(8,128)(2,1)} %fc2_h.1, bf16[192,256]{1,0:T(8,128)(2,1)} %bitcast.7, ...), custom_call_target="tpu_custom_call" | custom-call | tf_op jit(solution)/shard_map/step/pallas_call | solution.py:496
  52.9 2.4 %results.1 = (f32[64,128]{1,0:T(8,128)}, f32[32,8192]{1,0:T(8,128)}, f32[8,96,256]{2,1,0:T(8,128)}, f32[32,768]{1,0:T(8,128)}, f32[32,192]{1,0:T(8,128)}) custom-call(f32[64,128]{1,0:T(8,128)} %get-tuple-element.15.refs_0_, f32[32,8192]{1,0:T(8,128)} %get-tuple-element.16.refs_1_, f32[8,96,256]{2,1,0:T(8,128)} %get-tuple-element.17.refs_2_, ...), custom_call_target="tpu_custom_call" | custom-call | tf_op jit(solution)/shard_map/results/pallas_call | solution.py:516

commit v4 on v3

--- a/solution.py
+++ b/solution.py
@@ -29,7 +29,7 @@
 GH = 96
 GX = 16
 GA = 48
-SPLIT = 264
+SPLIT = 272
 FAR = (6, 2, 5, 7, 4, 1, 3)
 FAR_Z = (4, 3, 5, 2, 6, 1, 7)
 
@@ -48,18 +48,35 @@
     return value, slope
 
 
+def split_counts(counts):
+    upper = counts.astype(BF16)
+    return jnp.concatenate([upper, (counts - upper.astype(F32)).astype(BF16)], axis=0)
+
+
+def join_counts(parts):
+    return parts[0:CROW].astype(F32) + parts[CROW:2 * CROW].astype(F32)
+
+
+def add_sums(parts):
+    total = parts[0].astype(F32)
+    for part in parts[1:]:
+        total = total + part.astype(F32)
+    counts = split_counts(total[SROW:SROW + CROW] + total[SROW + CROW:SROW + 2 * CROW])
+    return total[0:SROW].astype(BF16), counts
+
+
 def dot(a, b, ca=1, cb=0):
     return lax.dot_general(a, b, (((ca,), (cb,)), ((), ())), preferred_element_type=F32)
 
 
 def kernel(
     tin_h, fc1_h, fc2_h, tok_h, enc_h, codes_h, cnt_h, sum_h, dec_h, head_h,
-    ncount_h, nsum_h, ghead_h, gdec_h, genc_h,
+    ncount_h, nsum_h, grads_h,
     tin, fc1, fc2, tok, enc, codes, cnt, esum, dec,
     th, tp, hid_t, q_rows, book, pred,
     hd, tp_r, z_s, z_r, s_s, s_r, s_z, s_all, dp_s, dp_r, dpre, g_s, g_r, g_z, g_all,
-    o_count, o_sum, o_head, o_dec, o_enc,
-    load_sem, out_sem,
+    o_count, o_sum,
+    ring, load_sem, out_sem,
     hd_ss, hd_rs, tp_ss, tp_rs, z_ss, z_rs, s1_ss, s1_rs, s2_ss, s2_rs, s3_ss, s3_rs,
     s4_ss, s4_rs, dp_ss, dp_rs, dr_ss, dr_rs, g1_ss, g1_rs, x1_ss, x1_rs, g2_ss, g2_rs,
     g3_ss, g3_rs,
@@ -86,17 +103,30 @@
 
     wrap = (zed * GRP + grp_index(4), over)
 
+    sent = []
+
     def remote(src, dst, ss, rs, dev):
-        return pltpu.make_async_remote_copy(
+        c = pltpu.make_async_remote_copy(
             src_ref=src, dst_ref=dst, send_sem=ss, recv_sem=rs,
             device_id=dev, device_id_type=MESH,
         )
+        sent.append(c)
+        return c
 
     barrier = pltpu.get_barrier_semaphore()
-    peers = [mp_peer(r) for r in (1, 2, 3)] + [wrap]
-    peers += [grp_peer(k) for k in range(1, GRP)] + [zed_peer(k) for k in range(1, ZED)]
-    for dev in peers:
-        pl.semaphore_signal(barrier, inc=1, device_id=dev, device_id_type=MESH)
+    yy = lax.rem(grp, 4)
+    row = zed * GRP + grp - yy
+    near = [mp_peer(r) for r in (1, 2, 3)] + [wrap]
+    near += [(row + lax.rem(yy + k, 4), mp) for k in (1, 3)] + [zed_peer(k) for k in (1, ZED - 1)]
+
+    def greet(sem):
+        for dev in near:
+            pl.semaphore_signal(sem, inc=1, device_id=dev, device_id_type=MESH)
+
+    def hear(sem):
+        pl.semaphore_wait(sem, len(near))
+
+    greet(barrier)
 
     loads = []
 
@@ -106,9 +136,9 @@
         loads.append(c)
         return c
 
-    l_tin = load(tin_h, tin)
     l_tok = load(tok_h, tok)
     l_enc = load(enc_h, enc)
+    l_tin = load(tin_h, tin)
     l_fc1 = [load(fc1_h.at[:, pl.ds(n * 256, 256)], fc1.at[n]) for n in range(4)]
     l_head = load(head_h, hd.at[mp])
     l_fc2 = [load(fc2_h.at[:, pl.ds(n * 256, 256)], fc2.at[n]) for n in range(4)]
@@ -127,7 +157,8 @@
     z_s[...] = dot(enc[...], tok[...]).astype(BF16)
     l_head.wait()
 
-    pl.semaphore_wait(barrier, len(peers))
+    hear(barrier)
+    greet(ring.at[0])
     c_z = [
         remote(z_s, z_r.at[r - 1], z_ss.at[r - 1], z_rs.at[r - 1], mp_peer(r)) for r in (2, 1, 3)
     ]
@@ -156,6 +187,9 @@
         c.start()
         c_tp.append(c)
 
+    hear(ring.at[0])
+    greet(ring.at[1])
+
     l_codes.wait()
     code = jnp.broadcast_to(codes[...], (32, ROWS))
     code_hi = jnp.right_shift(code, 7)
@@ -163,25 +197,24 @@
     lo_id = lax.broadcasted_iota(jnp.int32, (128, ROWS), 0)
     lo_hot = jnp.where(lo_id == code_lo, 1.0, 0.0).astype(BF16)
 
+    hear(ring.at[1])
+    greet(ring.at[2])
+
     for c in c_z:
-        c.wait()
+        c.wait_recv()
     z_t = z_s[...].astype(F32)
     for r in range(3):
         z_t = z_t + z_r[r].astype(F32)
-    z_upper = z_t.astype(BF16).astype(F32)
-    z_lower = z_t - z_upper
     for i in range(QHI // 2):
-        halves = []
-        for part in (z_upper, z_lower):
-            for j in range(2):
-                halves.append(jnp.where(code_hi == mp * QHI + i * 2 + j, part, 0.0))
-        both = dot(jnp.concatenate(halves, axis=0).astype(BF16), lo_hot, 1, 1)
-        s_s[i, 0:SROW] = both[0:SROW] + both[SROW:2 * SROW]
+        pair = [jnp.where(code_hi == mp * QHI + i * 2 + j, z_t, 0.0) for j in range(2)]
+        pair = jnp.concatenate(pair, axis=0).astype(BF16)
+        s_s[i, 0:SROW] = dot(pair, lo_hot, 1, 1).astype(BF16)
     hi_id = lax.broadcasted_iota(jnp.int32, (CROW, ROWS), 0) + mp * QHI
     hi_hot = jnp.where(hi_id == code_hi[0:CROW], 1.0, 0.0).astype(BF16)
-    counts = dot(hi_hot, lo_hot, 1, 1)
+    counts = split_counts(dot(hi_hot, lo_hot, 1, 1))
     for i in range(GRP):
-        s_s[i, SROW:SROW + CROW] = counts
+        s_s[i, SROW:SROW + 2 * CROW] = counts
+    hear(ring.at[2])
     c_s1 = []
     for k in FAR:
         c = remote(
@@ -211,10 +244,10 @@
     hidden, slope = gelu_and_slope(dot(q_rows[own_rows, :].astype(BF16), dec[...]))
     hidden = hidden.astype(BF16)
 
-    c_sib.wait()
+    c_sib.wait_recv()
     c_fwd = []
     for i in range(3):
-        c_wrap[i].wait()
+        c_wrap[i].wait_recv()
         rows = hd.at[over, cuts[i]]
         c = remote(rows, rows, hd_ss.at[4 + i], hd_rs.at[4 + i], (dp, sib))
         c.start()
@@ -222,11 +255,11 @@
     for b in (mp, sib, over):
         pred[b] = dot(hidden, hd[b])
     for c in c_fwd:
-        c.wait()
+        c.wait_recv()
     pred[sib_over] = dot(hidden, hd[sib_over])
 
     for c in c_tp:
-        c.wait()
+        c.wait_recv()
     target = []
     for n in range(4):
         t = tin[own_rows, n * 256:(n + 1) * 256].astype(F32) + tp[n, own_rows, :].astype(F32)
@@ -267,11 +300,10 @@
         c_dr.append(c)
 
     for c in c_s1:
-        c.wait()
-    s_part = s_s[grp]
-    for k in range(GRP - 1):
-        s_part = s_part + s_r[k]
-    s_z[zed] = s_part
+        c.wait_recv()
+    sums, counts = add_sums([s_s[grp]] + [s_r[k] for k in range(GRP - 1)])
+    s_z[zed, 0:SROW] = sums
+    s_z[zed, SROW:SROW + 2 * CROW] = counts
     c_s2 = []
     for k in FAR_Z:
         c = remote(s_z.at[zed], s_z.at[zed], s2_ss.at[k - 1], s2_rs.at[k - 1], zed_peer(k))
@@ -285,7 +317,7 @@
         ).astype(BF16)
 
     for c in c_dp:
-        c.wait()
+        c.wait_recv()
     grad = dot(hid_t[...], dp_r[...].reshape(ROWS, 256)).astype(BF16)
     for i in range(GRP):
         g_s[i, 0:GH] = grad[i * GH:(i + 1) * GH]
@@ -300,7 +332,7 @@
             c_g1[part].append(c)
 
     for c in c_dr:
-        c.wait()
+        c.wait_recv()
     dpre_all = dpre[...].reshape(ROWS, 768)
     dq_t = dot(dec[...], dpre_all, 1, 1)
     dz_t = (dq_t + 2.0 * BETA * (z_t - q_t)).astype(BF16)
@@ -340,7 +372,7 @@
     def gather(part):
         first, size = halves[part]
         for c in c_g2[part]:
-            c.wait()
+            c.wait_recv()
         g_part = g_z[0, first:first + size].astype(F32)
         for k in range(1, ZED):
             g_part = g_part + g_z[k, first:first + size].astype(F32)
@@ -352,17 +384,15 @@
             c_g3[part].append(c)
 
     for c in c_g1[0]:
-        c.wait()
+        c.wait_recv()
     along_z(0)
 
     for c in c_s2:
-        c.wait()
-    s_part = s_z[0]
-    for k in range(1, ZED):
-        s_part = s_part + s_z[k]
+        c.wait_recv()
+    sums, counts = add_sums([s_z[k] for k in range(ZED)])
     own_part = pl.ds(pl.multiple_of(grp * SROW, SROW), SROW)
-    s_all[mp, own_part] = s_part[0:SROW]
-    s_all[mp, pl.ds(GRP * SROW, CROW)] = s_part[SROW:SROW + CROW]
+    s_all[mp, own_part] = sums
+    s_all[mp, pl.ds(GRP * SROW, 2 * CROW)] = counts
     c_s3 = []
     for k in FAR:
         c = remote(
@@ -373,13 +403,13 @@
         c_s3.append(c)
 
     for c in c_g1[1] + c_x1:
-        c.wait()
+        c.wait_recv()
     along_z(1)
     gather(0)
 
     for c in c_s3:
-        c.wait()
-    parts = (pl.ds(0, SPLIT), pl.ds(SPLIT, GRP * SROW + CROW - SPLIT))
+        c.wait_recv()
+    parts = (pl.ds(0, SPLIT), pl.ds(SPLIT, GRP * SROW + 2 * CROW - SPLIT))
     c_over = []
     for i, dev in enumerate(((dp, over), wrap)):
         rows = s_all.at[mp, parts[i]]
@@ -392,14 +422,14 @@
     gather(1)
     c_last = []
     for i in range(2):
-        c_over[i].wait()
+        c_over[i].wait_recv()
         rows = s_all.at[over, parts[i]]
         c = remote(rows, rows, s4_ss.at[3 + i], s4_rs.at[3 + i], (dp, sib))
         c.start()
         c_last.append(c)
 
     for c in c_last + [c_near]:
-        c.wait()
+        c.wait_recv()
     outs = []
 
     def store(src, dst):
@@ -410,51 +440,64 @@
     for m in range(NMP):
         o_count[m * CROW:(m + 1) * CROW] = (
             DECAY * cnt[m * CROW:(m + 1) * CROW]
-            + (1.0 - DECAY) * s_all[m, GRP * SROW:GRP * SROW + CROW]
+            + (1.0 - DECAY) * join_counts(s_all[m, GRP * SROW:GRP * SROW + 2 * CROW])
         )
         for i in range(QHI):
             columns = slice((m * QHI + i) * 128, (m * QHI + i + 1) * 128)
             o_sum[:, columns] = DECAY * esum[:, columns] + (1.0 - DECAY) * s_all[
                 m, i * 32:(i + 1) * 32
-            ]
+            ].astype(F32)
     store(o_count, ncount_h)
     store(o_sum, nsum_h)
 
-    for part, rows in enumerate((slice(0, GA), slice(GA, GH))):
+    for part, (first, size) in enumerate(halves):
         for c in c_g3[part]:
-            c.wait()
-        for i in range(GRP):
-            o_head[i, rows] = g_all[i, rows].astype(F32)
-        store(o_head.at[:, rows], ghead_h.at[:, rows])
+            c.wait_recv()
+        rows = pl.ds(first, size)
+        store(g_all.at[:, rows], grads_h.at[:, rows])
+    for c in sent:
+        c.wait_send()
+    for c in outs:
+        c.wait()
+
+
+def results(
+    count_h, sum_h, grads_h, ncount_h, nsum_h, ghead_h, gdec_h, genc_h,
+    count, sums, grads, head, dec, enc, in_sem, out_sem,
+):
+    groups = [pl.ds(i * 2, 2) for i in range(GRP // 2)]
+    columns = [pl.ds(i * 2048, 2048) for i in range(4)]
+    ins = [(grads_h.at[g], grads.at[g]) for g in groups]
+    ins += [(sum_h.at[:, c], sums.at[:, c]) for c in columns] + [(count_h, count)]
+    ins = [pltpu.make_async_copy(*pair, in_sem.at[i]) for i, pair in enumerate(ins)]
+    for c in ins:
+        c.start()
+    outs = []
+
+    def store(src, dst):
+        c = pltpu.make_async_copy(src, dst, out_sem.at[len(outs)])
+        c.start()
+        outs.append(c)
+
+    for i, g in enumerate(groups):
+        ins[i].wait()
+        for j in (2 * i, 2 * i + 1):
+            head[j] = grads[j, 0:GH].astype(F32)
+        store(head.at[g], ghead_h.at[g])
+    for i, c in enumerate(columns):
+        ins[4 + i].wait()
+        store(sums.at[:, c], nsum_h.at[:, c])
+    ins[8].wait()
+    store(count, ncount_h)
     for n in range(3):
         for i in range(2):
-            o_dec[i * 16:(i + 1) * 16, n * 256:(n + 1) * 256] = g_all[
+            dec[i * 16:(i + 1) * 16, n * 256:(n + 1) * 256] = grads[
                 n * 2 + i, GH:GH + GX
             ].astype(F32)
-    store(o_dec, gdec_h)
+    store(dec, gdec_h)
     for i in range(2):
-        o_enc[i * 16:(i + 1) * 16] = g_all[6 + i, GH:GH + GX, 0:192].astype(F32)
-    store(o_enc, genc_h)
-    for c in outs:
-        c.wait()
-
-
-def copy_out(*refs):
-    arrays, results, buffers, (in_sem, out_sem) = refs[0:5], refs[5:10], refs[10:15], refs[15:]
-    pieces = [(1, (slice(None), pl.ds(i * 2048, 2048))) for i in range(4)]
-    pieces += [(2, (pl.ds(i * 2, 2),)) for i in range(4)]
-    pieces += [(i, (slice(None),)) for i in (0, 3, 4)]
-    ins = []
-    for i, (a, at) in enumerate(pieces):
-        c = pltpu.make_async_copy(arrays[a].at[at], buffers[a].at[at], in_sem.at[i])
-        c.start()
-        ins.append(c)
-    outs = []
-    for i, (a, at) in enumerate(pieces):
-        ins[i].wait()
-        c = pltpu.make_async_copy(buffers[a].at[at], results[a].at[at], out_sem.at[i])
-        c.start()
-        outs.append(c)
+        enc[i * 16:(i + 1) * 16] = grads[6 + i, GH:GH + GX, 0:192].astype(F32)
+    store(enc, genc_h)
     for c in outs:
         c.wait()
 
@@ -479,17 +522,16 @@
     exchanged = [
         vm((4, 768, 256), BF16), vm((3, 4, OWN, 256), BF16), vm((32, ROWS), BF16),
         vm((3, 32, ROWS), BF16),
-        vm((GRP, SROW + CROW, 128), F32), vm((GRP - 1, SROW + CROW, 128), F32),
-        vm((ZED, SROW + CROW, 128), F32), vm((NMP, GRP * SROW + CROW, 128), F32),
+        vm((GRP, SROW + 2 * CROW, 128), BF16), vm((GRP - 1, SROW + 2 * CROW, 128), BF16),
+        vm((ZED, SROW + 2 * CROW, 128), BF16), vm((NMP, GRP * SROW + 2 * CROW, 128), BF16),
         vm((4, OWN, 256), BF16), vm((4, OWN, 256), BF16), vm((4, OWN, 768), BF16),
         vm((GRP, GH + GX, 256), BF16), vm((GRP - 1, GH + GX, 256), BF16),
         vm((ZED, GH + GX, 256), BF16), vm((GRP, GH + GX, 256), BF16),
     ]
-    results = [
-        vm((HI, 128), F32), vm((32, 8192), F32), vm((GRP, GH, 256), F32), vm((32, 768), F32),
-        vm((32, 192), F32),
+    made = [
+        vm((HI, 128), F32), vm((32, 8192), F32),
     ]
-    semaphores = [sems(16), sems(6)]
+    semaphores = [pltpu.SemaphoreType.REGULAR((3,)), sems(16), sems(8)]
     semaphores += two(7) + two(3) + two(3) + two(7) + two(7) + two(7)
     semaphores += two(5) + two(3) + two(3) + two(2, 7) + two(7) + two(2, 7) + two(2, 7)
     anywhere = pl.BlockSpec(memory_space=pl.ANY)
@@ -498,13 +540,11 @@
         out_shape=(
             jax.ShapeDtypeStruct((HI, 128), F32),
             jax.ShapeDtypeStruct((32, 8192), F32),
-            jax.ShapeDtypeStruct((GRP, GH, 256), F32),
-            jax.ShapeDtypeStruct((32, 768), F32),
-            jax.ShapeDtypeStruct((32, 192), F32),
+            jax.ShapeDtypeStruct((GRP, GH + GX, 256), BF16),
         ),
         in_specs=[pl.BlockSpec(memory_space=pltpu.HBM)] * 10,
-        out_specs=(anywhere,) * 5,
-        scratch_shapes=local + exchanged + results + semaphores,
+        out_specs=(anywhere,) * 3,
+        scratch_shapes=local + exchanged + made + semaphores,
         compiler_params=pltpu.CompilerParams(
             collective_id=0, has_side_effects=True, vmem_limit_bytes=64 * 2**20
         ),
@@ -513,12 +553,15 @@
         teacher_in, teacher_fc1, teacher_fc2, tok_in.T, enc_proj.T, codes.reshape(1, ROWS),
         ema_count.reshape(HI, 128), ema_sum, dec_in, head,
     )
+    final = [(HI, 128), (32, 8192), (GRP, GH, 256), (32, 768), (32, 192)]
     outs = pl.pallas_call(
-        copy_out,
-        out_shape=tuple(jax.ShapeDtypeStruct(o.shape, o.dtype) for o in outs),
-        in_specs=[pl.BlockSpec(memory_space=pltpu.HBM)] * 5,
+        results,
+        out_shape=tuple(jax.ShapeDtypeStruct(shape, F32) for shape in final),
+        in_specs=[pl.BlockSpec(memory_space=pltpu.HBM)] * 3,
         out_specs=(pl.BlockSpec(memory_space=pltpu.HBM),) * 5,
-        scratch_shapes=[vm(o.shape, o.dtype) for o in outs] + two(11),
+        scratch_shapes=[vm(final[0], F32), vm(final[1], F32), vm((GRP, GH + GX, 256), BF16)]
+        + [vm(shape, F32) for shape in final[2:]]
+        + [sems(9), sems(11)],
         compiler_params=pltpu.CompilerParams(vmem_limit_bytes=64 * 2**20),
         name="results",
     )(*outs)

time: 55.5 us -> 55.8 us (level)
  no operation moved by 1% of the time
where the time goes in v4:
time: 55.8 us; the launch traced here: 55.7 us
  Pallas kernels  55.1 us (99%)
  between operations  0.64 us (1%)
    pallas_call x1, Pallas kernels, on_device(): pl.pallas_call(kernel, out_shape=(jax.ShapeDtypeStruct((HI, 128), F32), j...  52.7 us
    pallas_call x1, Pallas kernels, on_device(): pl.pallas_call(results, out_shape=tuple((jax.ShapeDtypeStruct(shape, F32)...  2.36 us

profile of v4, /device:TPU:1, one launch (start us, length us, event | category | flops | bytes accessed | tf_op | source)
XLA Modules:
  0.0 55.7 jit_solution(1267701053641995014)
XLA Ops:
  0.6 52.7 %step.1 = (f32[64,128]{1,0:T(8,128)}, f32[32,8192]{1,0:T(8,128)}, bf16[8,112,256]{2,1,0:T(8,128)(2,1)}) custom-call(bf16[256,1024]{1,0:T(8,128)(2,1)} %tin_h.1, bf16[1024,1024]{1,0:T(8,128)(2,1)} %fc1_h.1, bf16[1024,1024]{1,0:T(8,128)(2,1)} %fc2_h.1, bf16[192,256]{1,0:T(8,128)(2,1)} %bitcast.7, bf16[32,192]{1,0:T(8,128)(2,1)} %bitcast.9, s32[1,256]{1,0:T(1,128)} %bitcast.10, ...), custom_call_target="tpu_custom_call" | custom-call | tf_op jit(solution)/shard_map/step/pallas_call | solution.py:538
  53.3 2.4 %results.1 = (f32[64,128]{1,0:T(8,128)}, f32[32,8192]{1,0:T(8,128)}, f32[8,96,256]{2,1,0:T(8,128)}, f32[32,768]{1,0:T(8,128)}, f32[32,192]{1,0:T(8,128)}) custom-call(f32[64,128]{1,0:T(8,128)} %get-tuple-element.13.count_h, f32[32,8192]{1,0:T(8,128)} %get-tuple-element.14.sum_h, bf16[8,112,256]{2,1,0:T(8,128)(2,1)} %get-tuple-element.15.grads_h), custom_call_target="tpu_custom_call" | custom-call | tf_op jit(solution)/shard_map/results/pallas_call | solution.py:557

commit v5 on v4

v5 whole, which is shorter than its diff:
```python
import functools
import math

import jax
import jax.numpy as jnp
from jax import lax
from jax.experimental import pallas as pl
from jax.experimental.pallas import tpu as pltpu
from jax.sharding import PartitionSpec as P

DECAY = 0.5
BETA = 0.25
EPS = 1e-06
MESH = pl.DeviceIdType.MESH
F32 = jnp.float32
BF16 = jnp.bfloat16
GELU_A = math.sqrt(2.0 / math.pi)
GELU_B = 0.044715

NMP = 4
PARTS = 16
QUADS = 4
ROWS = 256
OWN = 64
HI = 64
QHI = 16
CD = 32
SROW = 48
GROW = 48
XROW = 16
OFFSETS = sorted(
    [(z, h, y) for z in range(2) for h in range(2) for y in range(4) if z + h + y > 0],
    key=lambda o: -(o[0] + 2 * o[1] + min(o[2], 4 - o[2])),
)

def gelu(x):
    return 0.5 * x * (1.0 + jnp.tanh(GELU_A * (x + GELU_B * (x * x * x))))


def gelu_and_slope(x):
    square = x * x
    t = jnp.tanh(GELU_A * (x + GELU_B * (square * x)))
    value = 0.5 * x * (1.0 + t)
    slope = 0.5 * (1.0 + t) + (0.5 * GELU_A) * x * (1.0 - t * t) * (
        1.0 + (3.0 * GELU_B) * square
    )
    return value, slope


def count_rows(counts):
    upper = counts.astype(BF16).astype(F32)
    row = lax.broadcasted_iota(jnp.int32, (SROW - CD, 128), 0)
    rest = jnp.where(row == 1, counts - upper, 0.0)
    return jnp.where(row == 0, upper, rest).astype(BF16)


def add_up(parts):
    total = parts[0].astype(F32)
    for part in parts[1:]:
        total = total + part.astype(F32)
    return total


def add_sums(parts):
    total = add_up(parts)
    counts = total[CD:CD + 1] + total[CD + 1:CD + 2]
    return total[0:CD].astype(BF16), count_rows(counts)


def dot(a, b, ca=1, cb=0):
    return lax.dot_general(a, b, (((ca,), (cb,)), ((), ())), preferred_element_type=F32)


def kernel(
    tin_h, fc1_h, fc2_h, tok_h, enc_h, codes_h, cnt_h, sum_h, dec_h, head_h,
    ncount_h, nsum_h, grads_h, small_h,
    tin, fc1, fc2, tok, enc, codes, cnt, esum, dec,
    th, tp, hid_t, q_rows, z_rows, book, pred,
    hd, tp_r, z_s, z_r, s_s, s_r, s_z, s_all, dp_s, dp_r, gd, dz,
    g_s, g_r, g_z, g_all, x_s, x_r, x_z, x_all,
    o_count, o_sum,
    ring, load_sem, out_sem,
    hd_ss, hd_rs, tp_ss, tp_rs, z_ss, z_rs, s1_ss, s1_rs, s2_ss, s2_rs, s3_ss, s3_rs,
    s4_ss, s4_rs, dp_ss, dp_rs, gd_ss, gd_rs, dz_ss, dz_rs, g1_ss, g1_rs, g2_ss, g2_rs,
    g3_ss, g3_rs, x1_ss, x1_rs, x2_ss, x2_rs, x3_ss, x3_rs,
):
    dp = lax.axis_index("dp")
    mp = lax.axis_index("mp")
    zed = lax.div(dp, 8)
    high = lax.rem(lax.div(dp, 4), 2)
    yy = lax.rem(dp, 4)
    odd = lax.rem(zed, 2)
    quad = lax.div(zed, 2)
    part = odd * 8 + high * 4 + yy
    sib = mp + 1 - 2 * lax.rem(mp, 2)
    over = lax.rem(mp + 2, NMP)
    sib_over = lax.rem(sib + 2, NMP)

    def mp_peer(r):
        return (dp, lax.rem(mp + r, NMP))

    def at(z, h, y):
        return z * 8 + h * 4 + y

    part_peers = []
    for dz_, dh_, dy_ in OFFSETS:
        odd_, high_, yy_ = lax.rem(odd + dz_, 2), lax.rem(high + dh_, 2), lax.rem(yy + dy_, 4)
        part_peers.append(((at(quad * 2 + odd_, high_, yy_), mp), at(odd_, high_, yy_)))

    def quad_peer(k):
        return (at(lax.rem(quad + k, QUADS) * 2 + odd, high, yy), mp)

    wrap = (at(zed, 1 - high, yy), over)

    sent = []

    def remote(src, dst, ss, rs, dev):
        c = pltpu.make_async_remote_copy(
            src_ref=src, dst_ref=dst, send_sem=ss, recv_sem=rs,
            device_id=dev, device_id_type=MESH,
        )
        sent.append(c)
        return c

    barrier = pltpu.get_barrier_semaphore()
    near = [mp_peer(r) for r in (1, 2, 3)] + [wrap]
    near += [(at(zed, high, lax.rem(yy + k, 4)), mp) for k in (1, 3)]
    near += [(at(lax.rem(zed + k, 8), high, yy), mp) for k in (1, 7)]

    def greet(sem):
        for dev in near:
            pl.semaphore_signal(sem, inc=1, device_id=dev, device_id_type=MESH)

    def hear(sem):
        pl.semaphore_wait(sem, len(near))

    greet(barrier)

    loads = []

    def load(src, dst):
        c = pltpu.make_async_copy(src, dst, load_sem.at[len(loads)])
        c.start()
        loads.append(c)
        return c

    l_tok = load(tok_h, tok)
    l_enc = load(enc_h, enc)
    l_head = load(head_h, hd.at[mp])
    l_tin = load(tin_h, tin)
    l_fc1 = [load(fc1_h.at[:, pl.ds(n * 256, 256)], fc1.at[n]) for n in range(4)]
    l_fc2 = [load(fc2_h.at[:, pl.ds(n * 256, 256)], fc2.at[n]) for n in range(4)]

    l_tok.wait()
    l_enc.wait()
    z_s[...] = dot(enc[...], tok[...]).astype(BF16)
    l_head.wait()

    hear(barrier)
    greet(ring.at[0])
    c_z = [
        remote(z_s, z_r.at[r - 1], z_ss.at[r - 1], z_rs.at[r - 1], mp_peer(r)) for r in (2, 1, 3)
    ]
    for c in c_z:
        c.start()
    cuts = (pl.ds(0, 256), pl.ds(256, 256), pl.ds(512, 256))
    c_wrap = []
    for i, dev in enumerate((wrap, wrap, (dp, over))):
        c_wrap.append(
            remote(hd.at[mp, cuts[i]], hd.at[mp, cuts[i]], hd_ss.at[i], hd_rs.at[i], dev)
        )
    for c in c_wrap:
        c.start()
    c_sib = remote(hd.at[mp], hd.at[mp], hd_ss.at[3], hd_rs.at[3], (dp, sib))
    c_sib.start()

    l_tin.wait()
    for n in range(4):
        l_fc1[n].wait()
        th[:, n * 256:(n + 1) * 256] = gelu(dot(tin[...], fc1[n])).astype(BF16)
    l_codes = load(codes_h, codes)
    l_cnt = load(cnt_h, cnt)
    l_sum = load(sum_h, esum)
    l_dec = load(dec_h, dec)

    for n in range(4):
        l_fc2[n].wait()
        tp[n] = dot(th[...], fc2[n]).astype(BF16)
    c_tp = []
    for r in (2, 1, 3):
        rows = pl.ds(pl.multiple_of(lax.rem(mp + r, NMP) * OWN, OWN), OWN)
        c = remote(
            tp.at[:, rows], tp_r.at[r - 1], tp_ss.at[r - 1], tp_rs.at[r - 1], mp_peer(r)
        )
        c.start()
        c_tp.append(c)

    hear(ring.at[0])
    greet(ring.at[1])

    l_codes.wait()
    code = jnp.broadcast_to(codes[...], (32, ROWS))
    code_hi = jnp.right_shift(code, 7)
    code_lo = jnp.broadcast_to(jnp.bitwise_and(codes[...], 127), (128, ROWS))
    lo_id = lax.broadcasted_iota(jnp.int32, (128, ROWS), 0)
    lo_hot = jnp.where(lo_id == code_lo, 1.0, 0.0).astype(BF16)

    hear(ring.at[1])
    greet(ring.at[2])

    for c in c_z:
        c.wait_recv()
    z_t = z_s[...].astype(F32)
    for r in range(3):
        z_t = z_t + z_r[r].astype(F32)
    hear(ring.at[2])
    greet(ring.at[3])
    hi_id = lax.broadcasted_iota(jnp.int32, (QHI, ROWS), 0) + mp * QHI
    hi_hot = jnp.where(hi_id == code_hi[0:QHI], 1.0, 0.0).astype(BF16)
    counts = dot(hi_hot, lo_hot, 1, 1)
    for i in range(QHI // 2):
        pair = [jnp.where(code_hi == mp * QHI + i * 2 + j, z_t, 0.0) for j in range(2)]
        pair = dot(jnp.concatenate(pair, axis=0).astype(BF16), lo_hot, 1, 1).astype(BF16)
        for j in range(2):
            s_s[i * 2 + j, 0:CD] = pair[j * CD:(j + 1) * CD]
            s_s[i * 2 + j, CD:SROW] = count_rows(counts[i * 2 + j:i * 2 + j + 1])
    hear(ring.at[3])

    def to_parts(src, dst, ss, rs):
        started = []
        for i, (dev, p) in enumerate(part_peers):
            c = remote(src.at[p], dst.at[i], ss.at[i], rs.at[i], dev)
            c.start()
            started.append(c)
        return started

    def to_quads(buf, ss, rs):
        started = []
        for k in (2, 1, 3):
            c = remote(buf.at[quad], buf.at[quad], ss.at[k - 1], rs.at[k - 1], quad_peer(k))
            c.start()
            started.append(c)
        return started

    def from_part(buf, ss, rs):
        started = []
        for i, (dev, _) in enumerate(part_peers):
            c = remote(buf.at[part], buf.at[part], ss.at[i], rs.at[i], dev)
            c.start()
            started.append(c)
        return started

    def arrive(copies):
        for c in copies:
            c.wait_recv()

    c_s1 = to_parts(s_s, s_r, s1_ss, s1_rs)
    z_rows[...] = z_t.T

    l_cnt.wait()
    l_sum.wait()
    l_dec.wait()
    lo_twice = jnp.concatenate([lo_hot, lo_hot], axis=0)
    inv = 1.0 / cnt[...]
    for h in range(HI):
        vector = esum[:, h * 128:(h + 1) * 128] * inv[h:h + 1, :]
        upper = vector.astype(BF16)
        book[h * 32:(h + 1) * 32, 0:128] = upper
        book[h * 32:(h + 1) * 32, 128:256] = (vector - upper.astype(F32)).astype(BF16)
    q_t = jnp.zeros((32, ROWS), F32)
    for i in range(HI // 8):
        found = dot(book[i * 256:(i + 1) * 256, :], lo_twice)
        for j in range(8):
            q_t = q_t + jnp.where(code_hi == i * 8 + j, found[j * 32:(j + 1) * 32], 0.0)
    q_rows[...] = q_t.T
    q_round_t = q_t.astype(BF16)
    own_rows = pl.ds(pl.multiple_of(mp * OWN, OWN), OWN)
    hidden, slope = gelu_and_slope(dot(q_rows[own_rows, :].astype(BF16), dec[...]))
    hidden = hidden.astype(BF16)

    c_sib.wait_recv()
    c_fwd = []
    for i in range(3):
        c_wrap[i].wait_recv()
        rows = hd.at[over, cuts[i]]
        c = remote(rows, rows, hd_ss.at[4 + i], hd_rs.at[4 + i], (dp, sib))
        c.start()
        c_fwd.append(c)
    for b in (mp, sib, over):
        pred[b] = dot(hidden, hd[b])
    for c in c_fwd:
        c.wait_recv()
    pred[sib_over] = dot(hidden, hd[sib_over])

    for c in c_tp:
        c.wait_recv()
    target = []
    for n in range(4):
        t = tin[own_rows, n * 256:(n + 1) * 256].astype(F32) + tp[n, own_rows, :].astype(F32)
        for r in range(3):
            t = t + tp_r[r, n].astype(F32)
        target.append(t)
    pp = jnp.zeros((OWN, 256), F32)
    pt = jnp.zeros((OWN, 256), F32)
    tt = jnp.zeros((OWN, 256), F32)
    for n in range(4):
        pp = pp + pred[n] * pred[n]
        pt = pt + pred[n] * target[n]
        tt = tt + target[n] * target[n]
    pp = jnp.sum(pp, axis=1, keepdims=True) + EPS
    pt = jnp.sum(pt, axis=1, keepdims=True)
    tt = jnp.sum(tt, axis=1, keepdims=True) + EPS
    inverse = 1.0 / (jnp.sqrt(pp) * jnp.sqrt(tt))
    scale = pt * inverse / pp
    for n in range(4):
        dp_s[n] = (scale * pred[n] - inverse * target[n]).astype(BF16)
    c_dp = []
    for r in (2, 1, 3):
        c = remote(
            dp_s.at[lax.rem(mp + r, NMP)], dp_r.at[mp], dp_ss.at[r - 1], dp_rs.at[r - 1],
            mp_peer(r),
        )
        c.start()
        c_dp.append(c)
    dp_r[mp] = dp_s[mp]
    dh = dot(dp_s[0], hd[0], 1, 1)
    for n in range(1, 4):
        dh = dh + dot(dp_s[n], hd[n], 1, 1)
    dpre = (dh * slope).astype(BF16)

    q_own = q_rows[own_rows, :]
    gd[mp] = dot(q_own.T.astype(BF16), dpre).astype(BF16)
    dq = dot(dpre, dec[...], 1, 1)
    dz[mp] = (dq + 2.0 * BETA * (z_rows[own_rows, :] - q_own)).astype(BF16)
    c_small = []
    for r in (2, 1, 3):
        for buf, ss, rs in ((gd, gd_ss, gd_rs), (dz, dz_ss, dz_rs)):
            c = remote(buf.at[mp], buf.at[mp], ss.at[r - 1], rs.at[r - 1], mp_peer(r))
            c.start()
            c_small.append(c)

    arrive(c_s1)
    sums, counts = add_sums([s_s[part]] + [s_r[i] for i in range(PARTS - 1)])
    s_z[quad, 0:CD] = sums
    s_z[quad, CD:SROW] = counts
    c_s2 = to_quads(s_z, s2_ss, s2_rs)

    dec_t = dec[...].astype(F32).T.astype(BF16)
    for n in range(3):
        hid_t[n * 256:(n + 1) * 256, :] = gelu(
            dot(dec_t[n * 256:(n + 1) * 256], q_round_t)
        ).astype(BF16)

    arrive(c_dp)
    grad = dot(hid_t[...], dp_r[...].reshape(ROWS, 256)).astype(BF16)
    for i in range(PARTS):
        g_s[i] = grad[i * GROW:(i + 1) * GROW]
    c_g1 = to_parts(g_s, g_r, g1_ss, g1_rs)

    arrive(c_small)
    grad_dec = add_up([gd[m] for m in range(NMP)]).astype(BF16)
    dz_t = dz[...].reshape(ROWS, CD).astype(F32).T.astype(BF16)
    grad_enc = dot(dz_t, tok[...], 1, 1).astype(BF16)
    for n in range(6):
        for i in range(2):
            x_s[n * 2 + i] = grad_dec[i * 16:(i + 1) * 16, n * 128:(n + 1) * 128]
    for i in range(2):
        x_s[12 + i] = grad_enc[i * 16:(i + 1) * 16, 0:128]
        x_s[14 + i, :, 0:64] = grad_enc[i * 16:(i + 1) * 16, 128:192]
        x_s[14 + i, :, 64:128] = jnp.zeros((XROW, 64), BF16)
    c_x1 = to_parts(x_s, x_r, x1_ss, x1_rs)

    arrive(c_s2)
    sums, counts = add_sums([s_z[k] for k in range(QUADS)])
    s_all[mp, part, 0:CD] = sums
    s_all[mp, part, CD:SROW] = counts
    c_s3 = from_part(s_all.at[mp], s3_ss, s3_rs)

    arrive(c_g1)
    g_z[quad] = add_up([g_s[part]] + [g_r[i] for i in range(PARTS - 1)]).astype(BF16)
    c_g2 = to_quads(g_z, g2_ss, g2_rs)
    arrive(c_x1)
    x_z[quad] = add_up([x_s[part]] + [x_r[i] for i in range(PARTS - 1)]).astype(BF16)
    c_x2 = to_quads(x_z, x2_ss, x2_rs)

    arrive(c_s3)
    halves = (pl.ds(0, PARTS // 2), pl.ds(PARTS // 2, PARTS // 2))
    c_over = []
    for i, dev in enumerate(((dp, over), wrap)):
        rows = s_all.at[mp, halves[i]]
        c = remote(rows, rows, s4_ss.at[i], s4_rs.at[i], dev)
        c.start()
        c_over.append(c)
    c_near = remote(s_all.at[mp], s_all.at[mp], s4_ss.at[2], s4_rs.at[2], (dp, sib))
    c_near.start()

    arrive(c_g2)
    g_all[part] = add_up([g_z[k] for k in range(QUADS)]).astype(BF16)
    c_g3 = from_part(g_all, g3_ss, g3_rs)
    arrive(c_x2)
    x_all[part] = add_up([x_z[k] for k in range(QUADS)]).astype(BF16)
    c_x3 = from_part(x_all, x3_ss, x3_rs)

    c_last = []
    for i in range(2):
        c_over[i].wait_recv()
        rows = s_all.at[over, halves[i]]
        c = remote(rows, rows, s4_ss.at[3 + i], s4_rs.at[3 + i], (dp, sib))
        c.start()
        c_last.append(c)

    arrive(c_last + [c_near])
    outs = []

    def store(src, dst):
        c = pltpu.make_async_copy(src, dst, out_sem.at[len(outs)])
        c.start()
        outs.append(c)

    for m in range(NMP):
        for i in range(QHI):
            h = m * QHI + i
            columns = slice(h * 128, (h + 1) * 128)
            o_sum[:, columns] = DECAY * esum[:, columns] + (1.0 - DECAY) * s_all[
                m, i, 0:CD
            ].astype(F32)
            rows = s_all[m, i, CD:SROW].astype(F32)
            o_count[h:h + 1] = DECAY * cnt[h:h + 1] + (1.0 - DECAY) * (rows[0:1] + rows[1:2])
    store(o_count, ncount_h)
    store(o_sum, nsum_h)

    arrive(c_g3)
    store(g_all, grads_h)
    arrive(c_x3)
    store(x_all, small_h)
    for c in sent:
        c.wait_send()
    for c in outs:
        c.wait()


def results(
    count_h, sum_h, grads_h, small_h, ncount_h, nsum_h, ghead_h, gdec_h, genc_h,
    count, sums, grads, small, head, dec, enc, in_sem, out_sem,
):
    parts = [pl.ds(i * 4, 4) for i in range(PARTS // 4)]
    columns = [pl.ds(i * 2048, 2048) for i in range(4)]
    ins = [(grads_h.at[p], grads.at[p]) for p in parts] + [(small_h, small)]
    ins += [(sum_h.at[:, c], sums.at[:, c]) for c in columns] + [(count_h, count)]
    ins = [pltpu.make_async_copy(*pair, in_sem.at[i]) for i, pair in enumerate(ins)]
    for c in ins:
        c.start()
    outs = []

    def store(src, dst):
        c = pltpu.make_async_copy(src, dst, out_sem.at[len(outs)])
        c.start()
        outs.append(c)

    for i, p in enumerate(parts):
        ins[i].wait()
        head[p] = grads[p].astype(F32)
        store(head.at[p], ghead_h.at[p])
    ins[4].wait()
    for n in range(6):
        for i in range(2):
            dec[i * 16:(i + 1) * 16, n * 128:(n + 1) * 128] = small[n * 2 + i].astype(F32)
    store(dec, gdec_h)
    for i in range(2):
        enc[i * 16:(i + 1) * 16, 0:128] = small[12 + i].astype(F32)
        enc[i * 16:(i + 1) * 16, 128:192] = small[14 + i, :, 0:64].astype(F32)
    store(enc, genc_h)
    for i, c in enumerate(columns):
        ins[5 + i].wait()
        store(sums.at[:, c], nsum_h.at[:, c])
    ins[9].wait()
    store(count, ncount_h)
    for c in outs:
        c.wait()


def on_device(
    teacher_in, teacher_fc1, teacher_fc2, tok_in, enc_proj, codes, ema_count, ema_sum, dec_in, head
):
    def sems(*shape):
        return pltpu.SemaphoreType.DMA(shape)

    def two(*shape):
        return [sems(*shape), sems(*shape)]

    vm = pltpu.VMEM
    local = [
        vm((ROWS, 1024), BF16), vm((4, 1024, 256), BF16), vm((4, 1024, 256), BF16),
        vm((192, ROWS), BF16), vm((CD, 192), BF16), vm((1, ROWS), jnp.int32),
        vm((HI, 128), F32), vm((CD, 8192), F32), vm((CD, 768), BF16),
        vm((ROWS, 1024), BF16), vm((4, ROWS, 256), BF16), vm((768, ROWS), BF16),
        vm((ROWS, CD), F32), vm((ROWS, CD), F32), vm((HI * CD, 256), BF16),
        vm((4, OWN, 256), F32),
    ]
    exchanged = [
        vm((4, 768, 256), BF16), vm((3, 4, OWN, 256), BF16), vm((CD, ROWS), BF16),
        vm((3, CD, ROWS), BF16),
        vm((PARTS, SROW, 128), BF16), vm((PARTS - 1, SROW, 128), BF16),
        vm((QUADS, SROW, 128), BF16), vm((NMP, PARTS, SROW, 128), BF16),
        vm((4, OWN, 256), BF16), vm((4, OWN, 256), BF16),
        vm((NMP, CD, 768), BF16), vm((NMP, OWN, CD), BF16),
        vm((PARTS, GROW, 256), BF16), vm((PARTS - 1, GROW, 256), BF16),
        vm((QUADS, GROW, 256), BF16), vm((PARTS, GROW, 256), BF16),
        vm((PARTS, XROW, 128), BF16), vm((PARTS - 1, XROW, 128), BF16),
        vm((QUADS, XROW, 128), BF16), vm((PARTS, XROW, 128), BF16),
    ]
    made = [vm((HI, 128), F32), vm((CD, 8192), F32)]
    semaphores = [pltpu.SemaphoreType.REGULAR((4,)), sems(16), sems(4)]
    semaphores += two(7) + two(3) + two(3) + two(15) + two(3) + two(15)
    semaphores += two(5) + two(3) + two(3) + two(3) + two(15) + two(3)
    semaphores += two(15) + two(15) + two(3) + two(15)
    anywhere = pl.BlockSpec(memory_space=pl.ANY)
    outs = pl.pallas_call(
        kernel,
        out_shape=(
            jax.ShapeDtypeStruct((HI, 128), F32),
            jax.ShapeDtypeStruct((32, 8192), F32),
            jax.ShapeDtypeStruct((PARTS, GROW, 256), BF16),
            jax.ShapeDtypeStruct((PARTS, XROW, 128), BF16),
        ),
        in_specs=[pl.BlockSpec(memory_space=pltpu.HBM)] * 10,
        out_specs=(anywhere,) * 4,
        scratch_shapes=local + exchanged + made + semaphores,
        compiler_params=pltpu.CompilerParams(
            collective_id=0, has_side_effects=True, vmem_limit_bytes=64 * 2**20
        ),
        name="step",
    )(
        teacher_in, teacher_fc1, teacher_fc2, tok_in.T, enc_proj.T, codes.reshape(1, ROWS),
        ema_count.reshape(HI, 128), ema_sum, dec_in, head,
    )
    final = [(HI, 128), (CD, 8192), (PARTS, GROW, 256), (CD, 768), (CD, 192)]
    outs = pl.pallas_call(
        results,
        out_shape=tuple(jax.ShapeDtypeStruct(shape, F32) for shape in final),
        in_specs=[pl.BlockSpec(memory_space=pltpu.HBM)] * 4,
        out_specs=(pl.BlockSpec(memory_space=pltpu.HBM),) * 5,
        scratch_shapes=[vm(final[0], F32), vm(final[1], F32)]
        + [vm((PARTS, GROW, 256), BF16), vm((PARTS, XROW, 128), BF16)]
        + [vm(shape, F32) for shape in final[2:]]
        + [sems(10), sems(11)],
        compiler_params=pltpu.CompilerParams(vmem_limit_bytes=64 * 2**20),
        name="results",
    )(*outs)
    return (outs[0].reshape(8192), outs[1], outs[2].reshape(768, 256), outs[3], outs[4].T)


def solution(mesh):
    placed = (
        P("dp", None),
        P(None, "mp"),
        P("mp", None),
        P("dp", "mp"),
        P("mp", None),
        P("dp"),
        P(),
        P(),
        P(),
        P(None, "mp"),
    )
    return jax.shard_map(
        on_device,
        mesh=mesh,
        in_specs=placed,
        out_specs=(P(), P(), P(None, "mp"), P(), P("mp", None)),
        check_vma=False,
    )
```

time: 55.8 us -> 51.9 us (0.930); the launches traced: 55.7 us -> 51.1 us
  Pallas kernels: 55.1 us -> 50.4 us
    pallas_call x1, Pallas kernels: 52.7 us -> 48.1 us  [on_device(): pl.pallas_call(kernel, out_shape=(jax.ShapeDtypeStruct((HI, 128), F32), j...]
where the time goes in v5:
time: 51.9 us; the launch traced here: 51.1 us
  Pallas kernels  50.4 us (97%)
  between operations  0.64 us (1%)
    pallas_call x1, Pallas kernels, on_device(): pl.pallas_call(kernel, out_shape=(jax.ShapeDtypeStruct((HI, 128), F32), j...  48.1 us
    pallas_call x1, Pallas kernels, on_device(): pl.pallas_call(results, out_shape=tuple((jax.ShapeDtypeStruct(shape, F32)...  2.36 us

profile of v5, /device:TPU:1, one launch (start us, length us, event | category | flops | bytes accessed | tf_op | source)
XLA Modules:
  0.0 51.1 jit_solution(1503550499668840132)
XLA Ops:
  0.6 48.1 %step.1 = (f32[64,128]{1,0:T(8,128)}, f32[32,8192]{1,0:T(8,128)}, bf16[16,48,256]{2,1,0:T(8,128)(2,1)}, bf16[16,16,128]{2,1,0:T(8,128)(2,1)}) custom-call(bf16[256,1024]{1,0:T(8,128)(2,1)} %tin_h.1, bf16[1024,1024]{1,0:T(8,128)(2,1)} %fc1_h.1, bf16[1024,1024]{1,0:T(8,128)(2,1)} %fc2_h.1, bf16[192,256]{1,0:T(8,128)(2,1)} %bitcast.7, bf16[32,192]{1,0:T(8,128)(2,1)} %bitcast.9, ...), custom_call_target="tpu_custom_call" | custom-call | tf_op jit(solution)/shard_map/step/pallas_call | solution.py:518
  48.7 2.4 %results.1 = (f32[64,128]{1,0:T(8,128)}, f32[32,8192]{1,0:T(8,128)}, f32[16,48,256]{2,1,0:T(8,128)}, f32[32,768]{1,0:T(8,128)}, f32[32,192]{1,0:T(8,128)}) custom-call(f32[64,128]{1,0:T(8,128)} %get-tuple-element.14.count_h, f32[32,8192]{1,0:T(8,128)} %get-tuple-element.15.sum_h, bf16[16,48,256]{2,1,0:T(8,128)(2,1)} %get-tuple-element.16.grads_h, ...), custom_call_target="tpu_custom_call" | custom-call | tf_op jit(solution)/shard_map/results/pallas_call | solution.py:538

commit v6 on v5

--- a/solution.py
+++ b/solution.py
@@ -76,7 +76,7 @@
     ncount_h, nsum_h, grads_h, small_h,
     tin, fc1, fc2, tok, enc, codes, cnt, esum, dec,
     th, tp, hid_t, q_rows, z_rows, book, pred,
-    hd, tp_r, z_s, z_r, s_s, s_r, s_z, s_all, dp_s, dp_r, gd, dz,
+    hd, tp_s, tp_r, z_s, z_r, s_s, s_r, s_z, s_all, dp_s, dp_r, gd, dz,
     g_s, g_r, g_z, g_all, x_s, x_r, x_z, x_all,
     o_count, o_sum,
     ring, load_sem, out_sem,
@@ -163,7 +163,7 @@
     ]
     for c in c_z:
         c.start()
-    cuts = (pl.ds(0, 256), pl.ds(256, 256), pl.ds(512, 256))
+    cuts = (pl.ds(0, 224), pl.ds(224, 224), pl.ds(448, 320))
     c_wrap = []
     for i, dev in enumerate((wrap, wrap, (dp, over))):
         c_wrap.append(
@@ -183,17 +183,25 @@
     l_sum = load(sum_h, esum)
     l_dec = load(dec_h, dec)
 
-    for n in range(4):
-        l_fc2[n].wait()
-        tp[n] = dot(th[...], fc2[n]).astype(BF16)
+    def rows_of(m):
+        return pl.ds(pl.multiple_of(m * OWN, OWN), OWN)
+
     c_tp = []
-    for r in (2, 1, 3):
-        rows = pl.ds(pl.multiple_of(lax.rem(mp + r, NMP) * OWN, OWN), OWN)
+
+    def to_core(cols, m, slot, i):
         c = remote(
-            tp.at[:, rows], tp_r.at[r - 1], tp_ss.at[r - 1], tp_rs.at[r - 1], mp_peer(r)
+            tp.at[cols, rows_of(m)], tp_r.at[slot, cols], tp_ss.at[i], tp_rs.at[i], (dp, sib)
         )
         c.start()
         c_tp.append(c)
+
+    pairs = (pl.ds(0, 2), pl.ds(2, 2))
+    for i in range(2):
+        for n in (2 * i, 2 * i + 1):
+            l_fc2[n].wait()
+            tp[n] = dot(th[...], fc2[n]).astype(BF16)
+        to_core(pairs[i], sib_over, 0, i)
+    to_core(pl.ds(0, 4), sib, 1, 2)
 
     hear(ring.at[0])
     greet(ring.at[1])
@@ -205,6 +213,17 @@
     lo_id = lax.broadcasted_iota(jnp.int32, (128, ROWS), 0)
     lo_hot = jnp.where(lo_id == code_lo, 1.0, 0.0).astype(BF16)
 
+    c_chip = []
+    for i in range(2):
+        c_tp[i].wait_recv()
+        for n in (2 * i, 2 * i + 1):
+            tp_s[n] = (tp[n, rows_of(over), :].astype(F32) + tp_r[0, n].astype(F32)).astype(BF16)
+        c = remote(
+            tp_s.at[pairs[i]], tp_r.at[2, pairs[i]], tp_ss.at[3 + i], tp_rs.at[3 + i], (dp, over)
+        )
+        c.start()
+        c_chip.append(c)
+
     hear(ring.at[1])
     greet(ring.at[2])
 
@@ -213,8 +232,6 @@
     z_t = z_s[...].astype(F32)
     for r in range(3):
         z_t = z_t + z_r[r].astype(F32)
-    hear(ring.at[2])
-    greet(ring.at[3])
     hi_id = lax.broadcasted_iota(jnp.int32, (QHI, ROWS), 0) + mp * QHI
     hi_hot = jnp.where(hi_id == code_hi[0:QHI], 1.0, 0.0).astype(BF16)
     counts = dot(hi_hot, lo_hot, 1, 1)
@@ -224,7 +241,8 @@
         for j in range(2):
             s_s[i * 2 + j, 0:CD] = pair[j * CD:(j + 1) * CD]
             s_s[i * 2 + j, CD:SROW] = count_rows(counts[i * 2 + j:i * 2 + j + 1])
-    hear(ring.at[3])
+    hear(ring.at[2])
+    greet(ring.at[3])
 
     def to_parts(src, dst, ss, rs):
         started = []
@@ -254,7 +272,6 @@
         for c in copies:
             c.wait_recv()
 
-    c_s1 = to_parts(s_s, s_r, s1_ss, s1_rs)
     z_rows[...] = z_t.T
 
     l_cnt.wait()
@@ -278,6 +295,9 @@
     hidden, slope = gelu_and_slope(dot(q_rows[own_rows, :].astype(BF16), dec[...]))
     hidden = hidden.astype(BF16)
 
+    hear(ring.at[3])
+    c_s1 = to_parts(s_s, s_r, s1_ss, s1_rs)
+
     c_sib.wait_recv()
     c_fwd = []
     for i in range(3):
@@ -292,13 +312,11 @@
         c.wait_recv()
     pred[sib_over] = dot(hidden, hd[sib_over])
 
-    for c in c_tp:
-        c.wait_recv()
+    arrive([c_tp[2]] + c_chip)
     target = []
     for n in range(4):
         t = tin[own_rows, n * 256:(n + 1) * 256].astype(F32) + tp[n, own_rows, :].astype(F32)
-        for r in range(3):
-            t = t + tp_r[r, n].astype(F32)
+        t = t + tp_r[1, n].astype(F32) + tp_r[2, n].astype(F32)
         target.append(t)
     pp = jnp.zeros((OWN, 256), F32)
     pt = jnp.zeros((OWN, 256), F32)
@@ -351,12 +369,6 @@
             dot(dec_t[n * 256:(n + 1) * 256], q_round_t)
         ).astype(BF16)
 
-    arrive(c_dp)
-    grad = dot(hid_t[...], dp_r[...].reshape(ROWS, 256)).astype(BF16)
-    for i in range(PARTS):
-        g_s[i] = grad[i * GROW:(i + 1) * GROW]
-    c_g1 = to_parts(g_s, g_r, g1_ss, g1_rs)
-
     arrive(c_small)
     grad_dec = add_up([gd[m] for m in range(NMP)]).astype(BF16)
     dz_t = dz[...].reshape(ROWS, CD).astype(F32).T.astype(BF16)
@@ -369,6 +381,12 @@
         x_s[14 + i, :, 0:64] = grad_enc[i * 16:(i + 1) * 16, 128:192]
         x_s[14 + i, :, 64:128] = jnp.zeros((XROW, 64), BF16)
     c_x1 = to_parts(x_s, x_r, x1_ss, x1_rs)
+
+    arrive(c_dp)
+    grad = dot(hid_t[...], dp_r[...].reshape(ROWS, 256)).astype(BF16)
+    for i in range(PARTS):
+        g_s[i] = grad[i * GROW:(i + 1) * GROW]
+    c_g1 = to_parts(g_s, g_r, g1_ss, g1_rs)
 
     arrive(c_s2)
     sums, counts = add_sums([s_z[k] for k in range(QUADS)])
@@ -498,7 +516,8 @@
         vm((4, OWN, 256), F32),
     ]
     exchanged = [
-        vm((4, 768, 256), BF16), vm((3, 4, OWN, 256), BF16), vm((CD, ROWS), BF16),
+        vm((4, 768, 256), BF16), vm((4, OWN, 256), BF16), vm((3, 4, OWN, 256), BF16),
+        vm((CD, ROWS), BF16),
         vm((3, CD, ROWS), BF16),
         vm((PARTS, SROW, 128), BF16), vm((PARTS - 1, SROW, 128), BF16),
         vm((QUADS, SROW, 128), BF16), vm((NMP, PARTS, SROW, 128), BF16),
@@ -511,7 +530,7 @@
     ]
     made = [vm((HI, 128), F32), vm((CD, 8192), F32)]
     semaphores = [pltpu.SemaphoreType.REGULAR((4,)), sems(16), sems(4)]
-    semaphores += two(7) + two(3) + two(3) + two(15) + two(3) + two(15)
+    semaphores += two(7) + two(5) + two(3) + two(15) + two(3) + two(15)
     semaphores += two(5) + two(3) + two(3) + two(3) + two(15) + two(3)
     semaphores += two(15) + two(15) + two(3) + two(15)
     anywhere = pl.BlockSpec(memory_space=pl.ANY)

time: 51.9 us -> 53.7 us (1.035); the launches traced: 51.1 us -> 53.5 us
  Pallas kernels: 50.4 us -> 52.9 us
    pallas_call x1, Pallas kernels: 48.1 us -> 50.5 us  [on_device(): pl.pallas_call(kernel, out_shape=(jax.ShapeDtypeStruct((HI, 128), F32), j...]
where the time goes in v6:
time: 53.7 us; the launch traced here: 53.5 us
  Pallas kernels  52.9 us (99%)
  between operations  0.64 us (1%)
    pallas_call x1, Pallas kernels, on_device(): pl.pallas_call(kernel, out_shape=(jax.ShapeDtypeStruct((HI, 128), F32), j...  50.5 us
    pallas_call x1, Pallas kernels, on_device(): pl.pallas_call(results, out_shape=tuple((jax.ShapeDtypeStruct(shape, F32)...  2.36 us

profile of v6, /device:TPU:1, one launch (start us, length us, event | category | flops | bytes accessed | tf_op | source)
XLA Modules:
  0.0 53.5 jit_solution(4916271944691263500)
XLA Ops:
  0.6 50.5 %step.1 = (f32[64,128]{1,0:T(8,128)}, f32[32,8192]{1,0:T(8,128)}, bf16[16,48,256]{2,1,0:T(8,128)(2,1)}, bf16[16,16,128]{2,1,0:T(8,128)(2,1)}) custom-call(bf16[256,1024]{1,0:T(8,128)(2,1)} %tin_h.1, bf16[1024,1024]{1,0:T(8,128)(2,1)} %fc1_h.1, bf16[1024,1024]{1,0:T(8,128)(2,1)} %fc2_h.1, bf16[192,256]{1,0:T(8,128)(2,1)} %bitcast.7, bf16[32,192]{1,0:T(8,128)(2,1)} %bitcast.9, ...), custom_call_target="tpu_custom_call" | custom-call | tf_op jit(solution)/shard_map/step/pallas_call | solution.py:537
  51.2 2.4 %results.1 = (f32[64,128]{1,0:T(8,128)}, f32[32,8192]{1,0:T(8,128)}, f32[16,48,256]{2,1,0:T(8,128)}, f32[32,768]{1,0:T(8,128)}, f32[32,192]{1,0:T(8,128)}) custom-call(f32[64,128]{1,0:T(8,128)} %get-tuple-element.14.count_h, f32[32,8192]{1,0:T(8,128)} %get-tuple-element.15.sum_h, bf16[16,48,256]{2,1,0:T(8,128)(2,1)} %get-tuple-element.16.grads_h, ...), custom_call_target="tpu_custom_call" | custom-call | tf_op jit(solution)/shard_map/results/pallas_call | solution.py:557

commit v7 on v6

--- a/solution.py
+++ b/solution.py
@@ -77,7 +77,7 @@
     tin, fc1, fc2, tok, enc, codes, cnt, esum, dec,
     th, tp, hid_t, q_rows, z_rows, book, pred,
     hd, tp_s, tp_r, z_s, z_r, s_s, s_r, s_z, s_all, dp_s, dp_r, gd, dz,
-    g_s, g_r, g_z, g_all, x_s, x_r, x_z, x_all,
+    g_s, g_r, g_z, g_sum, x_s, x_r, x_z, x_sum,
     o_count, o_sum,
     ring, load_sem, out_sem,
     hd_ss, hd_rs, tp_ss, tp_rs, z_ss, z_rs, s1_ss, s1_rs, s2_ss, s2_rs, s3_ss, s3_rs,
@@ -260,10 +260,10 @@
             started.append(c)
         return started
 
-    def from_part(buf, ss, rs):
+    def from_part(src, dst, ss, rs):
         started = []
         for i, (dev, _) in enumerate(part_peers):
-            c = remote(buf.at[part], buf.at[part], ss.at[i], rs.at[i], dev)
+            c = remote(src, dst.at[part], ss.at[i], rs.at[i], dev)
             c.start()
             started.append(c)
         return started
@@ -369,6 +369,12 @@
             dot(dec_t[n * 256:(n + 1) * 256], q_round_t)
         ).astype(BF16)
 
+    arrive(c_dp)
+    grad = dot(hid_t[...], dp_r[...].reshape(ROWS, 256)).astype(BF16)
+    for i in range(PARTS):
+        g_s[i] = grad[i * GROW:(i + 1) * GROW]
+    c_g1 = to_parts(g_s, g_r, g1_ss, g1_rs)
+
     arrive(c_small)
     grad_dec = add_up([gd[m] for m in range(NMP)]).astype(BF16)
     dz_t = dz[...].reshape(ROWS, CD).astype(F32).T.astype(BF16)
@@ -382,17 +388,11 @@
         x_s[14 + i, :, 64:128] = jnp.zeros((XROW, 64), BF16)
     c_x1 = to_parts(x_s, x_r, x1_ss, x1_rs)
 
-    arrive(c_dp)
-    grad = dot(hid_t[...], dp_r[...].reshape(ROWS, 256)).astype(BF16)
-    for i in range(PARTS):
-        g_s[i] = grad[i * GROW:(i + 1) * GROW]
-    c_g1 = to_parts(g_s, g_r, g1_ss, g1_rs)
-
     arrive(c_s2)
     sums, counts = add_sums([s_z[k] for k in range(QUADS)])
     s_all[mp, part, 0:CD] = sums
     s_all[mp, part, CD:SROW] = counts
-    c_s3 = from_part(s_all.at[mp], s3_ss, s3_rs)
+    c_s3 = from_part(s_all.at[mp, part], s_all.at[mp], s3_ss, s3_rs)
 
     arrive(c_g1)
     g_z[quad] = add_up([g_s[part]] + [g_r[i] for i in range(PARTS - 1)]).astype(BF16)
@@ -412,12 +412,21 @@
     c_near = remote(s_all.at[mp], s_all.at[mp], s4_ss.at[2], s4_rs.at[2], (dp, sib))
     c_near.start()
 
+    outs = []
+
+    def store(src, dst):
+        c = pltpu.make_async_copy(src, dst, out_sem.at[len(outs)])
+        c.start()
+        outs.append(c)
+
     arrive(c_g2)
-    g_all[part] = add_up([g_z[k] for k in range(QUADS)]).astype(BF16)
-    c_g3 = from_part(g_all, g3_ss, g3_rs)
+    g_sum[...] = add_up([g_z[k] for k in range(QUADS)]).astype(BF16)
+    c_g3 = from_part(g_sum, grads_h, g3_ss, g3_rs)
+    store(g_sum, grads_h.at[part])
     arrive(c_x2)
-    x_all[part] = add_up([x_z[k] for k in range(QUADS)]).astype(BF16)
-    c_x3 = from_part(x_all, x3_ss, x3_rs)
+    x_sum[...] = add_up([x_z[k] for k in range(QUADS)]).astype(BF16)
+    c_x3 = from_part(x_sum, small_h, x3_ss, x3_rs)
+    store(x_sum, small_h.at[part])
 
     c_last = []
     for i in range(2):
@@ -428,13 +437,6 @@
         c_last.append(c)
 
     arrive(c_last + [c_near])
-    outs = []
-
-    def store(src, dst):
-        c = pltpu.make_async_copy(src, dst, out_sem.at[len(outs)])
-        c.start()
-        outs.append(c)
-
     for m in range(NMP):
         for i in range(QHI):
             h = m * QHI + i
@@ -448,9 +450,7 @@
     store(o_sum, nsum_h)
 
     arrive(c_g3)
-    store(g_all, grads_h)
     arrive(c_x3)
-    store(x_all, small_h)
     for c in sent:
         c.wait_send()
     for c in outs:
@@ -524,9 +524,9 @@
         vm((4, OWN, 256), BF16), vm((4, OWN, 256), BF16),
         vm((NMP, CD, 768), BF16), vm((NMP, OWN, CD), BF16),
         vm((PARTS, GROW, 256), BF16), vm((PARTS - 1, GROW, 256), BF16),
-        vm((QUADS, GROW, 256), BF16), vm((PARTS, GROW, 256), BF16),
+        vm((QUADS, GROW, 256), BF16), vm((GROW, 256), BF16),
         vm((PARTS, XROW, 128), BF16), vm((PARTS - 1, XROW, 128), BF16),
-        vm((QUADS, XROW, 128), BF16), vm((PARTS, XROW, 128), BF16),
+        vm((QUADS, XROW, 128), BF16), vm((XROW, 128), BF16),
     ]
     made = [vm((HI, 128), F32), vm((CD, 8192), F32)]
     semaphores = [pltpu.SemaphoreType.REGULAR((4,)), sems(16), sems(4)]

time: 53.7 us -> 49.6 us (0.924)
  Pallas kernels: 52.9 us -> 48.4 us
    pallas_call x1, Pallas kernels: 50.5 us -> 46 us  [on_device(): pl.pallas_call(kernel, out_shape=(jax.ShapeDtypeStruct((HI, 128), F32), j...]
where the time goes in v7:
time: 49.6 us; the launch traced here: 49 us
  Pallas kernels  48.4 us (98%)
  between operations  0.64 us (1%)
    pallas_call x1, Pallas kernels, on_device(): pl.pallas_call(kernel, out_shape=(jax.ShapeDtypeStruct((HI, 128), F32), j...  46 us
    pallas_call x1, Pallas kernels, on_device(): pl.pallas_call(results, out_shape=tuple((jax.ShapeDtypeStruct(shape, F32)...  2.36 us

profile of v7, /device:TPU:1, one launch (start us, length us, event | category | flops | bytes accessed | tf_op | source)
XLA Modules:
  0.0 49.0 jit_solution(15643236238959999129)
XLA Ops:
  0.6 46.0 %step.1 = (f32[64,128]{1,0:T(8,128)}, f32[32,8192]{1,0:T(8,128)}, bf16[16,48,256]{2,1,0:T(8,128)(2,1)}, bf16[16,16,128]{2,1,0:T(8,128)(2,1)}) custom-call(bf16[256,1024]{1,0:T(8,128)(2,1)} %tin_h.1, bf16[1024,1024]{1,0:T(8,128)(2,1)} %fc1_h.1, bf16[1024,1024]{1,0:T(8,128)(2,1)} %fc2_h.1, bf16[192,256]{1,0:T(8,128)(2,1)} %bitcast.7, bf16[32,192]{1,0:T(8,128)(2,1)} %bitcast.9, ...), custom_call_target="tpu_custom_call" | custom-call | tf_op jit(solution)/shard_map/step/pallas_call | solution.py:537
  46.7 2.4 %results.1 = (f32[64,128]{1,0:T(8,128)}, f32[32,8192]{1,0:T(8,128)}, f32[16,48,256]{2,1,0:T(8,128)}, f32[32,768]{1,0:T(8,128)}, f32[32,192]{1,0:T(8,128)}) custom-call(f32[64,128]{1,0:T(8,128)} %get-tuple-element.14.count_h, f32[32,8192]{1,0:T(8,128)} %get-tuple-element.15.sum_h, bf16[16,48,256]{2,1,0:T(8,128)(2,1)} %get-tuple-element.16.grads_h, ...), custom_call_target="tpu_custom_call" | custom-call | tf_op jit(solution)/shard_map/results/pallas_call | solution.py:557

commit v8 on v7

--- a/solution.py
+++ b/solution.py
@@ -127,14 +127,16 @@
     near += [(at(zed, high, lax.rem(yy + k, 4)), mp) for k in (1, 3)]
     near += [(at(lax.rem(zed + k, 8), high, yy), mp) for k in (1, 7)]
 
-    def greet(sem):
-        for dev in near:
+    ahead = [near[1]] + near[3:]
+
+    def greet(sem, devices=ahead):
+        for dev in devices:
             pl.semaphore_signal(sem, inc=1, device_id=dev, device_id_type=MESH)
 
-    def hear(sem):
-        pl.semaphore_wait(sem, len(near))
-
-    greet(barrier)
+    def hear(sem, devices=ahead):
+        pl.semaphore_wait(sem, len(devices))
+
+    greet(barrier, near)
 
     loads = []
 
@@ -156,7 +158,7 @@
     z_s[...] = dot(enc[...], tok[...]).astype(BF16)
     l_head.wait()
 
-    hear(barrier)
+    hear(barrier, near)
     greet(ring.at[0])
     c_z = [
         remote(z_s, z_r.at[r - 1], z_ss.at[r - 1], z_rs.at[r - 1], mp_peer(r)) for r in (2, 1, 3)

time: 49.6 us -> 50.6 us (1.020)
  Pallas kernels: 48.4 us -> 49.8 us
    pallas_call x1, Pallas kernels: 46 us -> 47.5 us  [on_device(): pl.pallas_call(kernel, out_shape=(jax.ShapeDtypeStruct((HI, 128), F32), j...]
where the time goes in v8:
time: 50.6 us; the launch traced here: 50.5 us
  Pallas kernels  49.8 us (98%)
  between operations  0.64 us (1%)
    pallas_call x1, Pallas kernels, on_device(): pl.pallas_call(kernel, out_shape=(jax.ShapeDtypeStruct((HI, 128), F32), j...  47.5 us
    pallas_call x1, Pallas kernels, on_device(): pl.pallas_call(results, out_shape=tuple((jax.ShapeDtypeStruct(shape, F32)...  2.36 us

profile of v8, /device:TPU:1, one launch (start us, length us, event | category | flops | bytes accessed | tf_op | source)
XLA Modules:
  0.0 50.5 jit_solution(14959440322376352609)
XLA Ops:
  0.6 47.5 %step.1 = (f32[64,128]{1,0:T(8,128)}, f32[32,8192]{1,0:T(8,128)}, bf16[16,48,256]{2,1,0:T(8,128)(2,1)}, bf16[16,16,128]{2,1,0:T(8,128)(2,1)}) custom-call(bf16[256,1024]{1,0:T(8,128)(2,1)} %tin_h.1, bf16[1024,1024]{1,0:T(8,128)(2,1)} %fc1_h.1, bf16[1024,1024]{1,0:T(8,128)(2,1)} %fc2_h.1, bf16[192,256]{1,0:T(8,128)(2,1)} %bitcast.7, bf16[32,192]{1,0:T(8,128)(2,1)} %bitcast.9, ...), custom_call_target="tpu_custom_call" | custom-call | tf_op jit(solution)/shard_map/step/pallas_call | solution.py:539
  48.1 2.4 %results.1 = (f32[64,128]{1,0:T(8,128)}, f32[32,8192]{1,0:T(8,128)}, f32[16,48,256]{2,1,0:T(8,128)}, f32[32,768]{1,0:T(8,128)}, f32[32,192]{1,0:T(8,128)}) custom-call(f32[64,128]{1,0:T(8,128)} %get-tuple-element.14.count_h, f32[32,8192]{1,0:T(8,128)} %get-tuple-element.15.sum_h, bf16[16,48,256]{2,1,0:T(8,128)(2,1)} %get-tuple-element.16.grads_h, ...), custom_call_target="tpu_custom_call" | custom-call | tf_op jit(solution)/shard_map/results/pallas_call | solution.py:559
